TPU v7x, 256 devices: a whole 4x4x8 slice. The times are simulated.
256 devices in a mesh: user: 16 (over y, z_lo, core), item: 16 (over z_hi, x).
Axes of the slice: x: 4, y: 4, z: 8 (z_hi: 4, z_lo: 2; z = z_hi * 2 + z_lo), core: 2. Of those that a mesh axis runs over, the one named last changes fastest.
Arguments:
- user_states: bfloat16 [8192, 256], P('user'), may hold values from -240 to 240
- quot_rows: bfloat16 [16384, 256], P('item'), may hold values from -6 to 6
- rem_table: bfloat16 [4096, 256], replicated, may hold values from -6 to 6
- neg_rem: int32 [16384], P('item'), may hold values from 0 to 4095
- pos_quot: int32 [8192], P('user'), may hold values from 0 to 16383
- pos_rem: int32 [8192], P('user'), may hold values from 0 to 4095
Outputs:
- grad_users: float32 [8192, 256], P('user')
- grad_quot: float32 [16384, 256], P('item')
- grad_rem: float32 [4096, 256], replicated
All inputs are finite; a program needn't handle non-finite values.
Results may differ from a plain program's by a relative error of at most 0.0065.
The roundings to bfloat16 on the way count: a program that leaves them out, or rounds other values in their place, can miss the bound.
Values sent between devices are 32-bit elements; how exact they have to be, the bound alone decides.
A program may use at most 64 MiB of HBM per device.

v0:
```python
import jax
import jax.numpy as jnp
from jax import lax
from jax.sharding import PartitionSpec as P


def per_device(user_states, quot_rows, rem_table, neg_rem, pos_quot, pos_rem):
    f32 = jnp.float32
    width_d = user_states.shape[1]
    scale = width_d ** (-0.5)
    count = quot_rows.shape[0]
    first = lax.axis_index("item") * count
    rem_neg = rem_table[neg_rem]
    neg_emb = (quot_rows.astype(f32) * rem_neg.astype(f32)).astype(jnp.bfloat16)
    offset = pos_quot - first
    owned = (offset >= 0) & (offset < count)
    slot = jnp.clip(offset, 0, count - 1)
    quot_pos = quot_rows[slot]
    rem_pos = rem_table[pos_rem]
    pos_emb = jnp.where(owned[:, None], quot_pos.astype(f32) * rem_pos.astype(f32), 0.0).astype(
        jnp.bfloat16
    )
    pos_part = scale * jnp.sum(user_states.astype(f32) * pos_emb.astype(f32), axis=1)
    block_width = min(512, count)
    blocks = neg_emb.reshape(count // block_width, block_width, width_d)

    def score(block):
        return scale * lax.dot_general(
            user_states, block, (((1,), (1,)), ((), ())), preferred_element_type=f32
        )

    local_top = jnp.max(lax.map(lambda b: jnp.max(score(b), axis=1), blocks), axis=0)
    top_neg = lax.pmax(local_top, "item")
    local_total = jnp.sum(
        lax.map(lambda b: jnp.sum(jnp.exp(score(b) - top_neg[:, None]), axis=1), blocks), axis=0
    )
    total, pos_score = lax.psum((local_total, pos_part), "item")
    top = jnp.maximum(top_neg, pos_score)
    lse = top + jnp.log(total * jnp.exp(top_neg - top) + jnp.exp(pos_score - top))
    coef = scale * (jnp.exp(pos_score - lse) - 1.0)

    def backward(carry, block):
        probs = jnp.exp(score(block) - lse[:, None]).astype(jnp.bfloat16)
        carry = carry + scale * jnp.dot(probs, block, preferred_element_type=f32)
        grad_block = scale * lax.dot_general(
            probs, user_states, (((0,), (0,)), ((), ())), preferred_element_type=f32
        )
        return (carry, grad_block)

    user_part, grad_blocks = lax.scan(backward, jnp.zeros(user_states.shape, f32), blocks)
    user_part = user_part + coef[:, None] * pos_emb.astype(f32)
    grad_users = lax.psum(user_part, "item")
    grad_neg = grad_blocks.reshape(count, width_d)
    grad_pos = jnp.where(owned[:, None], coef[:, None] * user_states.astype(f32), 0.0)
    quot_part = grad_neg * rem_neg.astype(f32)
    quot_part = quot_part.at[slot].add(grad_pos * rem_pos.astype(f32))
    rem_rows = rem_table.shape[0]
    rem_part = jax.ops.segment_sum(grad_neg * quot_rows.astype(f32), neg_rem, rem_rows)
    rem_part = rem_part + jax.ops.segment_sum(grad_pos * quot_pos.astype(f32), pos_rem, rem_rows)
    grad_quot = lax.psum(quot_part, "user")
    grad_rem = lax.psum(rem_part, ("user", "item"))
    return (grad_users, grad_quot, grad_rem)


def solution(mesh):
    in_specs = (P("user", None), P("item", None), P(), P("item"), P("user"), P("user"))
    out_specs = (P("user", None), P("item", None), P())
    return jax.shard_map(
        per_device, mesh=mesh, in_specs=in_specs, out_specs=out_specs, check_vma=False
    )
```

profile of v0, /device:TPU:1, one launch (start us, length us, event | category | flops | bytes accessed | tf_op | source)
XLA Modules:
  0.0 703.2 jit_solution(8625004269256877880)
XLA Ops:
  7.2 0.8 compare_and_fusion
  9.5 0.7 fusion.37
  10.2 2.6 gather_fusion.2
  12.8 2.6 gather_fusion.1
  15.3 1.3 fusion.32
  16.6 5.0 gather_fusion
  21.6 2.0 fusion.27
  23.6 2.7 while.33
  23.6 1.3 fusion.63
  24.9 1.3 fusion.63
  26.3 41.1 %pmax.7 = f32[512]{0:T(512)S(1)} all-reduce(f32[512]{0:T(512)S(1)} %reduce_max.18), channel_id=1, replica_groups=mesh['user'=16,'item'=16] {'item'}, use_global_device_ids=true, to_apply=%region_4.5 | all-reduce | flops 512 | bytes 4096 | tf_op jit(solution)/shard_map/pmax | solution.py:33
  67.4 2.8 while.34
  67.4 1.3 fusion.66
  68.8 1.3 fusion.66
  70.2 32.1 %all-reduce = (f32[512]{0:T(512)S(1)}, f32[512]{0:T(512)S(1)}) all-reduce(f32[512]{0:T(512)S(1)} %broadcast_multiply_fusion, f32[512]{0:T(512)S(1)} %reduce_sum.28), channel_id=1, replica_groups=mesh['user'=16,'item'=16] {'item'}, use_global_device_ids=true, to_apply=%region_6.7 | all-reduce | flops 1024 | bytes 8192 | tf_op jit(solution)/shard_map/psum | solution.py:37
  102.3 8.3 %while.35 = (s32[]{:T(128)}, f32[512,256]{1,0:T(8,128)S(1)}, f32[2,512,256]{2,1,0:T(8,128)}, bf16[2,512,256]{2,1,0:T(8,128)(2,1)}, bf16[512,256]{1,0:T(8,128)(2,...) while((s32[]{:T(128)}, f32[512,256]{1,0:T(8,128)S(1)}, f32[2,512,256]{2,1,0:T(8,128)}, ...), condition=%wide.region_13.14_spmd.clone, body=%wide.region_12.13_spmd.clone.sunk | while | flops 403963904 | bytes 12585131 | solution.py:50
  102.4 1.4 fusion.73
  103.8 1.5 fusion.74
  105.6 1.0 copy-done.6
  106.5 1.4 fusion.73
  107.9 1.5 fusion.74
  109.7 1.0 copy-done.6
  110.7 2.3 convert_multiply_fusion.7
  113.0 2.9 convert_multiply_fusion.2
  116.0 6.4 scatter_custom_fusion
  122.4 11.8 %scatter_custom_fusion.1 = f32[4096,256]{1,0:T(8,128)} fusion(s32[1536]{0:T(1024)S(1)} %add_reduce_fusion, f32[]{:T(128)} %constant.38.clone.1, f32[512,256]{1,0:T(8,128)S(1)} %copy-done.4, f32[]{:T(128)} %constant.40.clone.1, f32[1024,256]{1,0:T(8,128)} %get-tuple-element.144), kind=kCustom, calls=%fused_computation.32 | custom fusion | flops 786432 | bytes 5767176 | tf_op jit(solution)/shard_map/add | solution.py:59
  134.3 144.2 %all-reduce.5.cloned.1.call-done = f32[512,256]{1,0:T(8,128)} async-done(((f32[512,256]{1,0:T(8,128)}), f32[512,256]{1,0:T(8,128)}) %all-reduce.5.cloned.1.call-update) | async-done | bytes 524304 | tf_op jit(solution)/shard_map/psum | solution.py:52
  278.5 136.1 %all-reduce.7.cloned.1.call-done = f32[1024,256]{1,0:T(8,128)} async-done(((f32[1024,256]{1,0:T(8,128)}), f32[1024,256]{1,0:T(8,128)}) %all-reduce.7.cloned.1.call-update) | async-done | bytes 1048592 | tf_op jit(solution)/shard_map/psum | solution.py:60
  414.5 273.5 %all-reduce.9.cloned.1.call-done = f32[4096,256]{1,0:T(8,128)} async-done(((f32[4096,256]{1,0:T(8,128)}), f32[4096,256]{1,0:T(8,128)}) %all-reduce.9.cloned.1.call-update) | async-done | bytes 4194320 | tf_op jit(solution)/shard_map/psum | solution.py:61
  688.0 1.9 copy.40
  689.9 2.3 copy.41
  692.2 4.5 copy.42
  (45 shorter events, 2.5 us)
Async XLA Ops:
  7.2 3.0 copy-start
  7.2 5.6 copy-start.1
  7.2 271.3 %all-reduce.5.cloned.1.call-start = ((), (), s32[]{:S(2)}) async-start(), calls=%async_computation | async-start | bytes 1048576 | tf_op jit(solution)/shard_map/psum | solution.py:52
  10.2 5.2 copy-start.2
  102.4 2.9 copy-start.5
  105.5 1.0 copy-start.6
  106.5 2.9 copy-start.5
  109.7 1.0 copy-start.6
  113.0 301.6 %all-reduce.7.cloned.1.call-start = ((), (), s32[]{:S(2)}) async-start(), calls=%async_computation.1 | async-start | bytes 2097152 | tf_op jit(solution)/shard_map/psum | solution.py:60
  113.0 2.9 copy-start.3
  115.9 6.4 copy-start.7
  115.9 6.4 copy-start.8
  115.9 6.5 copy-start.4
  122.3 565.7 %all-reduce.9.cloned.1.call-start = ((), (), s32[]{:S(2)}) async-start(), calls=%async_computation.2 | async-start | bytes 8388608 | tf_op jit(solution)/shard_map/psum | solution.py:61
Sparse Core Ops, SparseCore 0:
  113.1 165.3 all-reduce.4
  281.3 133.2 all-reduce.6
  420.6 267.3 all-reduce.8
where the time goes:
time: 705 us; the launch traced here: 703 us
  waiting for transfers between devices  554 us (79%)
  blocking collectives  73.2 us (10%)
  other arithmetic  29.6 us (4%)
  local copies, waits for them, and re-layouts  20.9 us (3%)
  between operations  13.8 us (2%)
  matrix products  11.5 us (2%)
    psum x1, waiting for transfers between devices, per_device(): grad_rem = lax.psum(rem_part, ('user', 'item'))  273 us
    psum x1, waiting for transfers between devices, per_device(): grad_users = lax.psum(user_part, 'item')  144 us
    psum x1, waiting for transfers between devices, per_device(): grad_quot = lax.psum(quot_part, 'user')  136 us
    pmax x1, blocking collectives, per_device(): top_neg = lax.pmax(local_top, 'item')  41.1 us
    psum x1, blocking collectives, per_device(): total, pos_score = lax.psum((local_total, pos_part), 'item')  32.1 us
  transfers between devices with their start and end apart: 3, of which 3 were waited for; matrix products, arithmetic and copies ran while one was open for 3% of the time, Pallas kernels for 0%

commit v1 on v0

v1 whole, which is shorter than its diff:
```python
import functools

import jax
import jax.numpy as jnp
from jax import lax
from jax.experimental import pallas as pl
from jax.experimental.pallas import tpu as pltpu
from jax.sharding import PartitionSpec as P

F32 = jnp.float32
BF16 = jnp.bfloat16
MESH = pl.DeviceIdType.MESH
D = 256
H = 128
NU = 512
NN = 1024
NR = 4096
SCALE = D ** (-0.5)


def coords():
    u = lax.axis_index("user")
    t = lax.axis_index("item")
    return t % 4, u // 4, (t // 4) * 2 + (u // 2) % 2, u % 2


def device(x, y, z, c):
    return (y * 4 + (z % 2) * 2 + c, (z // 2) * 4 + x)


def split_pair(v):
    hi = v.astype(BF16)
    lo = (v - hi.astype(F32)).astype(BF16)
    return hi, lo


def columns_of(row):
    return jnp.transpose(jnp.broadcast_to(row, (128, 128)))


def kernel(
    user, quot, rem, neg_rem, pos_quot, pos_rem,
    out_u, out_q, out_r,
    remneg, emb, rempos, qpos, pemb, st, pt, stat, stat_in, idx, idx_in, half, half_in,
    rhs, rhsq, gr, gq, gu, a1, a2, a3, b1, b2, b3, q1, q2, u1, u2,
    send, recv,
):
    x, y, z, c = coords()
    zh, zl = z // 2, z % 2
    t = zh * 4 + x
    sems = [0]

    def peer(dx=0, dy=0, dz=0, dc=0):
        return device((x + dx) % 4, (y + dy) % 4, (z + dz) % 8, (c + dc) % 2)

    def copy(src, dst, to):
        s = sems[0]
        sems[0] += 1
        return pltpu.make_async_remote_copy(
            src_ref=src, dst_ref=dst, send_sem=send.at[s], recv_sem=recv.at[s],
            device_id=to, device_id_type=MESH,
        )

    item_peers = [(dx, 0, dz, 0) for dz in (0, 2, 4, 6) for dx in range(4) if (dx, dz) != (0, 0)]
    z_peers = [(0, 0, dz, 0) for dz in (1, 3, 5, 7)]
    y_peers = [(0, dy, 0, 0) for dy in (1, 2, 3)]
    peers = item_peers + z_peers + y_peers + [(0, 0, 0, 1)]
    barrier = pltpu.get_barrier_semaphore()
    for p in peers:
        pl.semaphore_signal(barrier, inc=1, device_id=peer(*p), device_id_type=MESH)

    lanes_r = lax.broadcasted_iota(jnp.int32, (256, NR), 1).astype(F32)
    lanes_q = lax.broadcasted_iota(jnp.int32, (256, NN), 1).astype(F32)

    def picks(row_ref, first, shift, lanes):
        parts = []
        for k in range(2):
            at = pl.ds(pl.multiple_of(first + k * 128, 128), 128)
            parts.append(columns_of((row_ref[0:1, at] - shift).astype(F32)))
        col = jnp.concatenate(parts, axis=0)
        wide = jnp.concatenate([col] * (lanes.shape[1] // 128), axis=1)
        return jnp.where(wide == lanes, 1.0, 0.0).astype(BF16)

    def gather_neg(b, carry):
        r0 = pl.multiple_of(b * 256, 256)
        got = jnp.dot(picks(neg_rem, r0, 0, lanes_r), rem[...], preferred_element_type=F32)
        remneg[pl.ds(r0, 256), :] = got
        emb[pl.ds(r0, 256), :] = (quot[pl.ds(r0, 256), :].astype(F32) * got).astype(BF16)
        return carry

    lax.fori_loop(0, NN // 256, gather_neg, 0)
    first = t * NN

    def gather_pos(b, carry):
        r0 = pl.multiple_of(b * 256, 256)
        got_r = jnp.dot(picks(pos_rem, r0, 0, lanes_r), rem[...], preferred_element_type=F32)
        got_q = jnp.dot(picks(pos_quot, r0, first, lanes_q), quot[...], preferred_element_type=F32)
        rempos[pl.ds(r0, 256), :] = got_r
        qpos[pl.ds(r0, 256), :] = got_q
        pemb[pl.ds(r0, 256), :] = (got_q * got_r).astype(BF16).astype(F32)
        return carry

    lax.fori_loop(0, NU // 256, gather_pos, 0)
    idx[0:1, :] = pos_rem[...].astype(F32)
    idx[1:2, :] = (pos_quot[...] - first).astype(F32)

    def scores(b, top):
        r0 = pl.multiple_of(b * 256, 256)
        s = SCALE * lax.dot_general(
            emb[pl.ds(r0, 256), :], user[...], (((1,), (1,)), ((), ())), preferred_element_type=F32
        )
        st[pl.ds(r0, 256), :] = s
        return jnp.maximum(top, jnp.max(s.reshape(32, 8, NU), axis=0))

    top8 = lax.fori_loop(0, NN // 256, scores, jnp.full((8, NU), -jnp.inf, F32))
    top_row = jnp.max(top8, axis=0, keepdims=True)

    def totals(b, tot):
        r0 = pl.multiple_of(b * 256, 256)
        e = jnp.exp(st[pl.ds(r0, 256), :] - top_row)
        return tot + jnp.sum(e.reshape(32, 8, NU), axis=0)

    tot8 = lax.fori_loop(0, NN // 256, totals, jnp.zeros((8, NU), F32))
    tot_row = jnp.sum(tot8, axis=0, keepdims=True)
    for k in range(4):
        at = slice(k * 128, (k + 1) * 128)
        stat[k : k + 1, :] = top_row[:, at]
        stat[4 + k : 5 + k, :] = tot_row[:, at]
        prod = user[at, :].astype(F32) * pemb[at, :]
        prod = prod[:, :H] + prod[:, H:]
        stat[8 + k : 9 + k, :] = SCALE * jnp.sum(jnp.transpose(prod), axis=0, keepdims=True)

    pl.semaphore_wait(barrier, len(peers))
    stat_copies = [copy(stat, stat_in.at[n], peer(*p)) for n, p in enumerate(item_peers)]
    for cp in stat_copies:
        cp.start()
    idx_copy = copy(idx, idx_in, peer(dc=1))
    idx_copy.start()
    for cp in stat_copies:
        cp.wait_recv()
    tops = [stat[0:4, :]] + [stat_in[n, 0:4, :] for n in range(15)]
    top_neg = functools.reduce(jnp.maximum, tops)
    total = stat[4:8, :] * jnp.exp(tops[0] - top_neg)
    pos_score = stat[8:12, :]
    for n in range(15):
        total = total + stat_in[n, 4:8, :] * jnp.exp(tops[n + 1] - top_neg)
        pos_score = pos_score + stat_in[n, 8:12, :]
    top = jnp.maximum(top_neg, pos_score)
    lse = top + jnp.log(total * jnp.exp(top_neg - top) + jnp.exp(pos_score - top))
    coef = SCALE * (jnp.exp(pos_score - lse) - 1.0)
    lse_row = jnp.concatenate([lse[k : k + 1, :] for k in range(4)], axis=1)

    def backward(b, carry):
        r0 = pl.multiple_of(b * 256, 256)
        at = pl.ds(r0, 256)
        p = jnp.exp(st[at, :] - lse_row).astype(BF16)
        pt[at, :] = p
        g = SCALE * jnp.dot(p, user[...], preferred_element_type=F32)
        half[0, at, :] = g[:, :H]
        half[1, at, :] = g[:, H:]
        return carry

    lax.fori_loop(0, NN // 256, backward, 0)
    for k in range(4):
        at = slice(k * 128, (k + 1) * 128)
        col = columns_of(coef[k : k + 1, :])
        for h in range(2):
            cols = slice(h * H, (h + 1) * H)
            gp = col * user[at, cols].astype(F32)
            owned = jnp.where(idx_col_owned(idx, k), gp, 0.0)
            half[h, NN + k * 128 : NN + (k + 1) * 128, :] = owned * qpos[at, cols]
            half[h, NN + NU + k * 128 : NN + NU + (k + 1) * 128, :] = owned * rempos[at, cols]
            gu[at, cols] = col * pemb[at, cols]
    half_copy = copy(half.at[1 - c], half_in, peer(dc=1))
    half_copy.start()

    def users(b, carry):
        at = pl.ds(pl.multiple_of(b * 256, 256), 256)
        g = lax.dot_general(
            pt[at, :], emb[at, :], (((0,), (0,)), ((), ())), preferred_element_type=F32
        )
        gu[...] += SCALE * g
        return carry

    lax.fori_loop(0, NN // 256, users, 0)

    def rows(first_row, count):
        return pl.ds(pl.multiple_of(first_row, 8), count)

    u_x = []
    for d in (1, 3, 2):
        cp = copy(gu.at[rows(((x + d) % 4) * 128, 128)], u1.at[d - 1], peer(dx=d))
        cp.start()
        u_x.append(cp)

    idx_copy.wait()
    half_copy.wait_recv()
    first_half = c == 0

    def pair(b, carry):
        at = pl.ds(pl.multiple_of(b * 256, 256), 256)
        g = half[c, at, :] + half_in[at, :]
        q = jnp.where(first_half, quot[at, :H].astype(F32), quot[at, H:].astype(F32))
        hi, lo = split_pair(g * q)
        rhs[at, :H] = hi
        rhs[at, H:] = lo
        rn = jnp.where(first_half, remneg[at, :H], remneg[at, H:])
        gq[at, :] = g * rn
        return carry

    lax.fori_loop(0, NN // 256, pair, 0)
    for base, src in ((0, half.at[c]), (NU, half_in)):
        hi, lo = split_pair(src[NN : NN + NU, :])
        rhs[NN + base : NN + base + NU, :H] = hi
        rhs[NN + base : NN + base + NU, H:] = lo
        hi, lo = split_pair(src[NN + NU : NN + 2 * NU, :])
        rhsq[base : base + NU, :H] = hi
        rhsq[base : base + NU, H:] = lo

    slots = jnp.concatenate([idx[1:2, :], idx_in[1:2, :]], axis=1)
    down_q = lax.broadcasted_iota(jnp.int32, (256, 2 * NU), 0).astype(F32)
    q_y = {}
    for d in (2, 1, 3, 0):
        r0 = ((y + d) % 4) * 256
        at = rows(r0, 256)
        pick = jnp.where(down_q + lax.convert_element_type(r0, F32) == slots, 1.0, 0.0).astype(BF16)
        g = jnp.dot(pick, rhsq[...], preferred_element_type=F32)
        gq[at, :] += g[:, :H] + g[:, H:]
        if d:
            q_y[d] = copy(gq.at[at], q1.at[d - 1], peer(dy=d))
            q_y[d].start()

    which = jnp.concatenate([neg_rem[...].astype(F32), idx[0:1, :], idx_in[0:1, :]], axis=1)
    down_r = lax.broadcasted_iota(jnp.int32, (256, NN + 2 * NU), 0).astype(F32)

    def make(r0):
        def step(b, carry):
            at0 = r0 + b * 256
            shift = lax.convert_element_type(at0, F32)
            pick = jnp.where(down_r == which - shift, 1.0, 0.0).astype(BF16)
            g = jnp.dot(pick, rhs[...], preferred_element_type=F32)
            gr[pl.ds(pl.multiple_of(at0, 256), 256), :] = g[:, :H] + g[:, H:]
            return carry

        lax.fori_loop(0, 2, step, 0)

    a_x, b_y = {}, {}
    for d in (2, 1, 3, 0):
        ra = ((x + d) % 4) * 512
        make(ra)
        if d:
            a_x[d] = copy(gr.at[rows(ra, 512)], a1.at[d - 1], peer(dx=d))
            a_x[d].start()
        rb = 2048 + ((y + d) % 4) * 512
        make(rb)
        if d:
            b_y[d] = copy(gr.at[rows(rb, 512)], b1.at[d - 1], peer(dy=d))
            b_y[d].start()

    def reduce(dst, r0, count, slots_ref, copies, n):
        for cp in copies:
            cp.wait_recv()
        v = dst[rows(r0, count), :]
        for k in range(n):
            v = v + slots_ref[k]
        dst[rows(r0, count), :] = v

    def start_all(cps):
        for cp in cps:
            cp.start()
        return cps

    ru = x * 128
    reduce(gu, ru, 128, u1, u_x, 3)
    u_z = start_all([
        copy(gu.at[rows(ru + ((zh + d) % 4) * 32, 32)], u2.at[d - 1], peer(dz=2 * d)) for d in (1, 3, 2)
    ])
    rq = y * 256
    reduce(gq, rq, 256, q1, q_y.values(), 3)
    q_z = start_all([copy(gq.at[rows(rq + (1 - zl) * 128, 128)], q2.at[0], peer(dz=1 - 2 * zl))])

    ra, rb = x * 512, 2048 + y * 512
    reduce(gr, ra, 512, a1, a_x.values(), 3)
    a_y = start_all([
        copy(gr.at[rows(ra + ((y + d) % 4) * 128, 128)], a2.at[d - 1], peer(dy=d)) for d in (2, 1, 3)
    ])
    reduce(gr, rb, 512, b1, b_y.values(), 3)
    b_x = start_all([
        copy(gr.at[rows(rb + ((x + d) % 4) * 128, 128)], b2.at[d - 1], peer(dx=d)) for d in (2, 1, 3)
    ])

    ru2 = ru + zh * 32
    for cp in u_z:
        cp.wait_recv()
    out_u[rows(ru2, 32), :] = gu[rows(ru2, 32), :] + u2[0] + u2[1] + u2[2]
    u_bz = start_all([
        copy(out_u.at[rows(ru2, 32)], out_u.at[rows(ru2, 32)], peer(dz=2 * d)) for d in (1, 3, 2)
    ])
    rq2 = rq + zl * 128
    q_z[0].wait_recv()
    out_q[c, rows(rq2, 128), :] = gq[rows(rq2, 128), :] + q2[0]
    q_bz = start_all([
        copy(out_q.at[c, rows(rq2, 128)], out_q.at[c, rows(rq2, 128)], peer(dz=1 - 2 * zl))
    ])

    ra2, rb2 = ra + y * 128, rb + x * 128
    reduce(gr, ra2, 128, a2, a_y, 3)
    z_order = (4, 3, 5, 2, 6, 1, 7)
    a_z = start_all([
        copy(gr.at[rows(ra2 + ((z + d) % 8) * 16, 16)], a3.at[d - 1], peer(dz=d)) for d in z_order
    ])
    reduce(gr, rb2, 128, b2, b_x, 3)
    b_z = start_all([
        copy(gr.at[rows(rb2 + ((z + d) % 8) * 16, 16)], b3.at[d - 1], peer(dz=d)) for d in z_order
    ])

    for cp in u_bz:
        cp.wait_recv()
    u_bx = start_all([
        copy(out_u.at[rows(ru, 128)], out_u.at[rows(ru, 128)], peer(dx=d)) for d in (2, 1, 3)
    ])
    q_bz[0].wait_recv()
    q_by = start_all([
        copy(out_q.at[c, rows(rq, 256)], out_q.at[c, rows(rq, 256)], peer(dy=d)) for d in (2, 1, 3)
    ])
    q_c = start_all([copy(out_q.at[c, rows(rq, 256)], out_q.at[c, rows(rq, 256)], peer(dc=1))])

    def finish(copies, r0, slots_ref):
        for cp in copies:
            cp.wait_recv()
        v = gr[rows(r0, 16), :]
        for k in range(7):
            v = v + slots_ref[k]
        out_r[c, rows(r0, 16), :] = v
        return start_all([
            copy(out_r.at[c, rows(r0, 16)], out_r.at[c, rows(r0, 16)], peer(dz=d)) for d in z_order
        ])

    a_bz = finish(a_z, ra2 + z * 16, a3)
    b_bz = finish(b_z, rb2 + z * 16, b3)

    def back(r0, count, axis):
        at = rows(r0, count)
        sent = [
            copy(out_r.at[c, at], out_r.at[c, at], peer(**{axis: d})) for d in (2, 1, 3)
        ]
        start_all(sent)
        return sent

    def over(r0, count):
        at = rows(r0, count)
        return start_all([copy(out_r.at[c, at], out_r.at[c, at], peer(dc=1))])

    for cp in a_bz:
        cp.wait_recv()
    a_by = back(ra2, 128, "dy")
    for cp in b_bz:
        cp.wait_recv()
    b_bx = back(rb2, 128, "dx")
    pairs = over(ra2, 128) + over(rb2, 128)
    for cp in a_by:
        cp.wait_recv()
    a_bx = back(ra, 512, "dx")
    for cp in b_bx:
        cp.wait_recv()
    b_by = back(rb, 512, "dy")
    for d in (2, 1, 3):
        pairs += over(x * 512 + ((y - d) % 4) * 128, 128)
        pairs += over(2048 + y * 512 + ((x - d) % 4) * 128, 128)
    for d, cp in zip((2, 1, 3), q_by):
        cp.wait_recv()
        q_c += over_q(out_q, copy, peer, c, rows, ((y - d) % 4) * 256)
    for k in (1, 2, 0):
        d = (2, 1, 3)[k]
        a_bx[k].wait_recv()
        pairs += over(((x - d) % 4) * 512, 512)
        b_by[k].wait_recv()
        pairs += over(2048 + ((y - d) % 4) * 512, 512)
    for cp in u_bx:
        cp.wait_recv()
    for cp in q_c + pairs:
        cp.wait_recv()
    sent = stat_copies + [half_copy] + u_x + list(q_y.values()) + list(a_x.values()) + list(b_y.values())
    sent += u_z + q_z + a_y + b_x + u_bz + q_bz + a_z + b_z + u_bx + q_by + q_c
    sent += a_bz + b_bz + a_by + b_bx + a_bx + b_by + pairs
    for cp in sent:
        cp.wait_send()


def idx_col_owned(idx, k):
    col = columns_of(idx[1:2, k * 128 : (k + 1) * 128])
    return (col >= 0.0) & (col < float(NN))


def over_q(out_q, copy, peer, c, rows, r0):
    at = rows(r0, 256)
    cp = copy(out_q.at[c, at], out_q.at[c, at], peer(dc=1))
    cp.start()
    return [cp]


COPIES = 140


def per_device(user_states, quot_rows, rem_table, neg_rem, pos_quot, pos_rem):
    vmem = pl.BlockSpec(memory_space=pltpu.VMEM)
    out_u, out_q, out_r = pl.pallas_call(
        kernel,
        out_shape=(
            jax.ShapeDtypeStruct((NU, D), F32),
            jax.ShapeDtypeStruct((2, NN, H), F32),
            jax.ShapeDtypeStruct((2, NR, H), F32),
        ),
        in_specs=[vmem] * 6,
        out_specs=(vmem, vmem, vmem),
        scratch_shapes=[
            pltpu.VMEM((NN, D), F32),
            pltpu.VMEM((NN, D), BF16),
            pltpu.VMEM((NU, D), F32),
            pltpu.VMEM((NU, D), F32),
            pltpu.VMEM((NU, D), F32),
            pltpu.VMEM((NN, NU), F32),
            pltpu.VMEM((NN, NU), BF16),
            pltpu.VMEM((12, 128), F32),
            pltpu.VMEM((15, 12, 128), F32),
            pltpu.VMEM((2, NU), F32),
            pltpu.VMEM((2, NU), F32),
            pltpu.VMEM((2, NN + 2 * NU, H), F32),
            pltpu.VMEM((NN + 2 * NU, H), F32),
            pltpu.VMEM((NN + 2 * NU, D), BF16),
            pltpu.VMEM((2 * NU, D), BF16),
            pltpu.VMEM((NR, H), F32),
            pltpu.VMEM((NN, H), F32),
            pltpu.VMEM((NU, D), F32),
            pltpu.VMEM((3, 512, H), F32),
            pltpu.VMEM((3, 128, H), F32),
            pltpu.VMEM((7, 16, H), F32),
            pltpu.VMEM((3, 512, H), F32),
            pltpu.VMEM((3, 128, H), F32),
            pltpu.VMEM((7, 16, H), F32),
            pltpu.VMEM((3, 256, H), F32),
            pltpu.VMEM((1, 128, H), F32),
            pltpu.VMEM((3, 128, D), F32),
            pltpu.VMEM((3, 32, D), F32),
            pltpu.SemaphoreType.DMA((COPIES,)),
            pltpu.SemaphoreType.DMA((COPIES,)),
        ],
        compiler_params=pltpu.CompilerParams(
            collective_id=0, has_side_effects=True, vmem_limit_bytes=56 << 20
        ),
        cost_estimate=pl.CostEstimate(flops=12 << 30, bytes_accessed=9 << 20, transcendentals=1 << 20),
        name="sampled_softmax_grads",
    )(
        user_states, quot_rows, rem_table,
        neg_rem.reshape(1, NN), pos_quot.reshape(1, NU), pos_rem.reshape(1, NU),
    )
    grad_quot = jnp.swapaxes(out_q, 0, 1).reshape(NN, D)
    grad_rem = jnp.swapaxes(out_r, 0, 1).reshape(NR, D)
    return out_u, grad_quot, grad_rem


def solution(mesh):
    in_specs = (P("user", None), P("item", None), P(), P("item"), P("user"), P("user"))
    out_specs = (P("user", None), P("item", None), P())
    return jax.shard_map(
        per_device, mesh=mesh, in_specs=in_specs, out_specs=out_specs, check_vma=False
    )
```

time: 705 us -> 101 us (0.14)
  waiting for transfers between devices: 554 us -> 0 us
  Pallas kernels: 0 us -> 85.3 us
  blocking collectives: 73.2 us -> 0 us
  other arithmetic: 29.6 us -> 0 us
  between operations: 13.8 us -> 0.65 us
  matrix products: 11.5 us -> 0 us
    psum x3 -> x0, waiting for transfers between devices: 554 us -> none  [the longest x1 273 us: per_device(): grad_rem = lax.psum(rem_part, ('user', 'item'))]
    pallas_call x0 -> x1, Pallas kernels: none -> 85.3 us  [per_device(): pl.pallas_call(kernel, out_shape=(jax.ShapeDtypeStruct((NU, D), F32), jax...]
    pmax x1 -> x0, blocking collectives: 41.1 us -> none  [per_device(): top_neg = lax.pmax(local_top, 'item')]
    psum x1 -> x0, blocking collectives: 32.1 us -> none  [per_device(): total, pos_score = lax.psum((local_total, pos_part), 'item')]
    add x1 -> x0, other arithmetic: 11.8 us -> none  [per_device(): rem_part + jax.ops.segment_sum(grad_pos * quot_pos.astype(f32), pos_rem,...]
    dot_general x10 -> x0, matrix products: 11.5 us -> none  [the longest x6 8.04 us: score(): lax.dot_general(user_states, block, (((1,), (1,)), ((), ())), preferred_e...]
    gather x3 -> x0, local copies, waits for them, and re-layouts: 10.1 us -> none  [the longest x1 4.98 us: per_device(): rem_neg = rem_table[neg_rem]]
    transpose x0 -> x2, local copies, waits for them, and re-layouts: none -> 7.16 us  [the longest x1 5.6 us: per_device(): grad_rem = jnp.swapaxes(out_r, 0, 1).reshape(NR, D)]
  transfers between devices with their start and end apart: 3 -> 0, of which waited for: 3 -> 0; matrix products, arithmetic and copies ran while one was open for 3% -> 0% of each run, Pallas kernels for 0% -> 0%
where the time goes in v1:
time: 101 us
  Pallas kernels  85.3 us (84%)
  local copies, waits for them, and re-layouts  14.9 us (15%)
    pallas_call x1, Pallas kernels, per_device(): pl.pallas_call(kernel, out_shape=(jax.ShapeDtypeStruct((NU, D), F32), jax...  85.3 us
    unnamed x5, local copies, waits for them, and re-layouts  7.75 us
    transpose x1, local copies, waits for them, and re-layouts, per_device(): grad_rem = jnp.swapaxes(out_r, 0, 1).reshape(NR, D)  5.6 us

profile of v1, /device:TPU:1, one launch (start us, length us, event | category | flops | bytes accessed | tf_op | source)
XLA Modules:
  0.0 100.9 jit_solution(14253401875823114036)
XLA Ops:
  0.6 85.3 %sampled_softmax_grads.1 = (f32[512,256]{1,0:T(8,128)}, f32[2,1024,128]{2,1,0:T(8,128)}, f32[2,4096,128]{2,1,0:T(8,128)}) custom-call(bf16[512,256]{1,0:T(8,128)(2,1)} %user.1, bf16[1024,256]{1,0:T(8,128)(2,1)} %quot.1, bf16[4096,256]{1,0:T(8,128)(2,1)} %rem.1, s32[1,1024]{1,0:T(1,128)} %bitcast.11, s32[1,512]{1,0:T(1,128)} %bitcast.12, s32[1,512]{1,0:T(1,128)} %bitcast.13), custom_call_target="tpu_custom_call" | custom-call | flops 12884901888 | bytes 9437184 | tf_op jit(solution)/shard_map/sampled_softmax_grads/pallas_call | solution.py:407
  86.0 1.6 %copy.9 = f32[1024,2,128]{0,2,1:T(8,128)S(1)} copy(f32[1024,2,128]{2,0,1:T(8,128)} %bitcast.10) | data formatting | bytes 2097152 | tf_op jit(solution)/shard_map/transpose | solution.py:457
  87.5 1.3 %copy.11 = f32[1024,256]{1,0:T(8,128)} copy(f32[1024,256]{0,1:T(8,128)S(1)} %bitcast.9) | data formatting | bytes 2097152
  88.9 5.6 %copy.10 = f32[4096,2,128]{0,2,1:T(8,128)} copy(f32[4096,2,128]{2,0,1:T(8,128)} %bitcast.8) | data formatting | bytes 8388608 | tf_op jit(solution)/shard_map/transpose | solution.py:458
  94.5 0.0 copy-start
  94.5 5.7 %copy.12 = f32[4096,256]{1,0:T(8,128)} copy(f32[4096,256]{0,1:T(8,128)} %bitcast.7) | data formatting | bytes 8388608
  100.1 0.0 copy-done
  100.1 0.8 copy.14
Async XLA Ops:
  94.5 5.7 %copy-start = (f32[512,256]{1,0:T(8,128)S(1)}, f32[512,256]{1,0:T(8,128)}, u32[]{:S(2)}) copy-start(f32[512,256]{1,0:T(8,128)} %get-tuple-element.15) | copy-start | bytes 1572868

commit v2 on v1

v2 whole, which is shorter than its diff:
```python
import functools

import jax
import jax.numpy as jnp
from jax import lax
from jax.experimental import pallas as pl
from jax.experimental.pallas import tpu as pltpu
from jax.sharding import PartitionSpec as P

F32 = jnp.float32
BF16 = jnp.bfloat16
MESH = pl.DeviceIdType.MESH
D = 256
H = 128
NU = 512
NN = 1024
NR = 4096
SCALE = D ** (-0.5)


def coords():
    u = lax.axis_index("user")
    t = lax.axis_index("item")
    return t % 4, u // 4, (t // 4) * 2 + (u // 2) % 2, u % 2


def device(x, y, z, c):
    return (y * 4 + (z % 2) * 2 + c, (z // 2) * 4 + x)


def split_pair(v):
    hi = v.astype(BF16)
    lo = (v - hi.astype(F32)).astype(BF16)
    return hi, lo


def columns_of(row):
    return jnp.transpose(jnp.broadcast_to(row, (128, 128)))


def kernel(
    user_hbm, quot_hbm, rem_hbm, neg_rem_hbm, pos_quot_hbm, pos_rem_hbm,
    out_u, out_q, out_r,
    user, quot, rem, neg_rem, pos_quot, pos_rem,
    remneg, emb, rempos, qpos, pemb, st, pt, stat, stat_in, idx, idx_in, half, half_in,
    rhs, rhsq, gr, gq, gu, first_in, second_in, third_in, q1, q2, u1, u2,
    load, send, recv,
):
    x, y, z, c = coords()
    zh, zl = z // 2, z % 2
    t = zh * 4 + x
    mine = pl.ds(pl.multiple_of(c * H, H), H)
    others = pl.ds(pl.multiple_of((1 - c) * H, H), H)

    def peer(dx=0, dy=0, dz=0, dc=0):
        return device((x + dx) % 4, (y + dy) % 4, (z + dz) % 8, (c + dc) % 2)

    item_peers = [(dx, 0, dz, 0) for dz in (0, 2, 4, 6) for dx in range(4) if (dx, dz) != (0, 0)]
    z_peers = [(0, 0, dz, 0) for dz in (1, 3, 5, 7)]
    y_peers = [(0, dy, 0, 0) for dy in (1, 2, 3)]
    peers = item_peers + z_peers + y_peers + [(0, 0, 0, 1)]
    barrier = pltpu.get_barrier_semaphore()
    for p in peers:
        pl.semaphore_signal(barrier, inc=1, device_id=peer(*p), device_id_type=MESH)

    loads = []
    for n, (src, dst) in enumerate((
        (neg_rem_hbm, neg_rem), (rem_hbm, rem), (quot_hbm, quot),
        (pos_rem_hbm, pos_rem), (pos_quot_hbm, pos_quot), (user_hbm, user),
    )):
        loads.append(pltpu.make_async_copy(src, dst, load.at[n]))
        loads[-1].start()

    sent = {}
    recvs = [0]

    def slot():
        recvs[0] += 1
        return recvs[0] - 1

    def go(src, dst, to, s, r, size):
        pltpu.make_async_remote_copy(
            src_ref=src, dst_ref=dst, send_sem=send.at[s], recv_sem=recv.at[r],
            device_id=to, device_id_type=MESH,
        ).start()
        sent[s] = sent.get(s, 0) + size

    def landed(ref, r):
        pltpu.make_async_remote_copy(
            src_ref=ref, dst_ref=ref, send_sem=send.at[0], recv_sem=recv.at[r],
            device_id=peer(dc=1), device_id_type=MESH,
        ).wait_recv()

    def left(ref, s):
        pltpu.make_async_remote_copy(
            src_ref=ref, dst_ref=ref, send_sem=send.at[s], recv_sem=recv.at[0],
            device_id=peer(dc=1), device_id_type=MESH,
        ).wait_send()

    def rows(first_row, count):
        return pl.ds(pl.multiple_of(first_row, 8), count)

    lanes_r = lax.broadcasted_iota(jnp.int32, (256, NR), 1).astype(F32)
    lanes_q = lax.broadcasted_iota(jnp.int32, (256, NN), 1).astype(F32)

    def picks(row_ref, first, shift, lanes):
        parts = []
        for k in range(2):
            at = pl.ds(pl.multiple_of(first + k * 128, 128), 128)
            parts.append(columns_of((row_ref[0:1, at] - shift).astype(F32)))
        col = jnp.concatenate(parts, axis=0)
        wide = jnp.concatenate([col] * (lanes.shape[1] // 128), axis=1)
        return jnp.where(wide == lanes, 1.0, 0.0).astype(BF16)

    def gather_neg(b, carry):
        r0 = pl.multiple_of(b * 256, 256)
        got = jnp.dot(picks(neg_rem, r0, 0, lanes_r), rem[...], preferred_element_type=F32)
        remneg[pl.ds(r0, 256), :] = got
        emb[pl.ds(r0, 256), :] = (quot[pl.ds(r0, 256), :].astype(F32) * got).astype(BF16)
        return carry

    for n in (0, 1, 2):
        loads[n].wait()
    lax.fori_loop(0, NN // 256, gather_neg, 0)
    first = t * NN

    def gather_pos(b, carry):
        r0 = pl.multiple_of(b * 256, 256)
        got_r = jnp.dot(picks(pos_rem, r0, 0, lanes_r), rem[...], preferred_element_type=F32)
        got_q = jnp.dot(picks(pos_quot, r0, first, lanes_q), quot[...], preferred_element_type=F32)
        rempos[pl.ds(r0, 256), :] = got_r
        qpos[pl.ds(r0, 256), :] = got_q
        pemb[pl.ds(r0, 256), :] = (got_q * got_r).astype(BF16).astype(F32)
        return carry

    for n in (3, 4, 5):
        loads[n].wait()
    lax.fori_loop(0, NU // 256, gather_pos, 0)
    idx[0:1, :] = pos_rem[...].astype(F32)
    idx[1:2, :] = (pos_quot[...] - first).astype(F32)

    def scores(b, top):
        r0 = pl.multiple_of(b * 256, 256)
        s = SCALE * lax.dot_general(
            emb[pl.ds(r0, 256), :], user[...], (((1,), (1,)), ((), ())), preferred_element_type=F32
        )
        st[pl.ds(r0, 256), :] = s
        return jnp.maximum(top, jnp.max(s.reshape(32, 8, NU), axis=0))

    top8 = lax.fori_loop(0, NN // 256, scores, jnp.full((8, NU), -jnp.inf, F32))
    top_row = jnp.max(top8, axis=0, keepdims=True)

    def totals(b, tot):
        r0 = pl.multiple_of(b * 256, 256)
        e = jnp.exp(st[pl.ds(r0, 256), :] - top_row)
        return tot + jnp.sum(e.reshape(32, 8, NU), axis=0)

    tot8 = lax.fori_loop(0, NN // 256, totals, jnp.zeros((8, NU), F32))
    tot_row = jnp.sum(tot8, axis=0, keepdims=True)
    for k in range(4):
        at = slice(k * 128, (k + 1) * 128)
        stat[k : k + 1, :] = top_row[:, at]
        stat[4 + k : 5 + k, :] = tot_row[:, at]
        prod = user[at, :].astype(F32) * pemb[at, :]
        prod = prod[:, :H] + prod[:, H:]
        stat[8 + k : 9 + k, :] = SCALE * jnp.sum(jnp.transpose(prod), axis=0, keepdims=True)

    pl.semaphore_wait(barrier, len(peers))
    r_stat, r_idx, r_half = slot(), slot(), slot()
    for n, p in enumerate(item_peers):
        go(stat, stat_in.at[n], peer(*p), 0, r_stat, 12)
    go(idx, idx_in, peer(dc=1), 1, r_idx, 8)
    landed(stat_in, r_stat)
    tops = [stat[0:4, :]] + [stat_in[n, 0:4, :] for n in range(15)]
    top_neg = functools.reduce(jnp.maximum, tops)
    total = stat[4:8, :] * jnp.exp(tops[0] - top_neg)
    pos_score = stat[8:12, :]
    for n in range(15):
        total = total + stat_in[n, 4:8, :] * jnp.exp(tops[n + 1] - top_neg)
        pos_score = pos_score + stat_in[n, 8:12, :]
    top = jnp.maximum(top_neg, pos_score)
    lse = top + jnp.log(total * jnp.exp(top_neg - top) + jnp.exp(pos_score - top))
    coef = SCALE * (jnp.exp(pos_score - lse) - 1.0)
    lse_row = jnp.concatenate([lse[k : k + 1, :] for k in range(4)], axis=1)

    def backward(b, carry):
        r0 = pl.multiple_of(b * 256, 256)
        at = pl.ds(r0, 256)
        p = jnp.exp(st[at, :] - lse_row).astype(BF16)
        pt[at, :] = p
        g = SCALE * jnp.dot(p, user[...], preferred_element_type=F32)
        half[0, at, :] = g[:, :H]
        half[1, at, :] = g[:, H:]
        return carry

    lax.fori_loop(0, NN // 256, backward, 0)
    for k in range(4):
        at = slice(k * 128, (k + 1) * 128)
        col = columns_of(coef[k : k + 1, :])
        slot_col = columns_of(idx[1:2, at])
        owned = (slot_col >= 0.0) & (slot_col < float(NN))
        for h in range(2):
            cols = slice(h * H, (h + 1) * H)
            gp = jnp.where(owned, col * user[at, cols].astype(F32), 0.0)
            half[h, NN + k * 128 : NN + (k + 1) * 128, :] = gp * qpos[at, cols]
            half[h, NN + NU + k * 128 : NN + NU + (k + 1) * 128, :] = gp * rempos[at, cols]
            gu[at, cols] = col * pemb[at, cols]
    go(half.at[1 - c], half_in, peer(dc=1), 2, r_half, NN + 2 * NU)

    def users(b, carry):
        at = pl.ds(pl.multiple_of(b * 256, 256), 256)
        g = lax.dot_general(
            pt[at, :], emb[at, :], (((0,), (0,)), ((), ())), preferred_element_type=F32
        )
        gu[...] += SCALE * g
        return carry

    lax.fori_loop(0, NN // 256, users, 0)
    r_ux = slot()
    for d in (1, 3, 2):
        go(gu.at[rows(((x + d) % 4) * 128, 128)], u1.at[d - 1], peer(dx=d), 3, r_ux, 256)

    landed(idx_in, r_idx)
    landed(half_in, r_half)
    first_half = c == 0

    def pair(b, carry):
        at = pl.ds(pl.multiple_of(b * 256, 256), 256)
        g = half[c, at, :] + half_in[at, :]
        q = jnp.where(first_half, quot[at, :H].astype(F32), quot[at, H:].astype(F32))
        hi, lo = split_pair(g * q)
        rhs[at, :H] = hi
        rhs[at, H:] = lo
        rn = jnp.where(first_half, remneg[at, :H], remneg[at, H:])
        gq[at, :] = g * rn
        return carry

    lax.fori_loop(0, NN // 256, pair, 0)
    for base, src in ((0, half.at[c]), (NU, half_in)):
        hi, lo = split_pair(src[NN : NN + NU, :])
        rhs[NN + base : NN + base + NU, :H] = hi
        rhs[NN + base : NN + base + NU, H:] = lo
        hi, lo = split_pair(src[NN + NU : NN + 2 * NU, :])
        rhsq[base : base + NU, :H] = hi
        rhsq[base : base + NU, H:] = lo

    slots = jnp.concatenate([idx[1:2, :], idx_in[1:2, :]], axis=1)
    down_q = lax.broadcasted_iota(jnp.int32, (256, 2 * NU), 0).astype(F32)
    r_qy = slot()
    for d in (2, 1, 3, 0):
        r0 = ((y + d) % 4) * 256
        at = rows(r0, 256)
        pick = jnp.where(down_q + lax.convert_element_type(r0, F32) == slots, 1.0, 0.0).astype(BF16)
        g = jnp.dot(pick, rhsq[...], preferred_element_type=F32)
        gq[at, :] += g[:, :H] + g[:, H:]
        if d:
            go(gq.at[at], q1.at[d - 1], peer(dy=d), 4, r_qy, 256)

    which = jnp.concatenate([neg_rem[...].astype(F32), idx[0:1, :], idx_in[0:1, :]], axis=1)
    down_r = lax.broadcasted_iota(jnp.int32, (256, NN + 2 * NU), 0).astype(F32)
    axes = {"x": x, "y": y}
    order = (2, 1, 3, 0)
    parts = [(0, "x", "y"), (1, "y", "x"), (2, "x", "y"), (3, "y", "x")]
    r_part = [{k: slot() for k in ("one", "two", "three", "z", "s1", "s2", "s3", "f1", "f2", "f3")} for _ in parts]
    r_pair = slot()

    def towards(axis, d):
        return peer(**{"d" + axis: d})

    def place(axis, d=0):
        return (axes[axis] + d) % 4

    def one(n, d):
        p, fst, snd = parts[n]
        r0 = p * 1024 + place(fst, d) * 256
        pick = jnp.where(down_r == which - lax.convert_element_type(r0, F32), 1.0, 0.0).astype(BF16)
        g = jnp.dot(pick, rhs[...], preferred_element_type=F32)
        gr[rows(r0, 256), :] = g[:, :H] + g[:, H:]
        if d:
            go(gr.at[rows(r0, 256)], first_in.at[n, d - 1], towards(fst, d), 5 + n, r_part[n]["one"], 256)

    def fold(dst, r0, count, slots_ref, n):
        v = dst[rows(r0, count), :]
        for k in range(n):
            v = v + slots_ref[k]
        return v

    def base1(n):
        p, fst, snd = parts[n]
        return p * 1024 + place(fst) * 256

    def base2(n):
        return base1(n) + place(parts[n][2]) * 64

    def base3(n):
        return base2(n) + z * 8

    def two(n):
        p, fst, snd = parts[n]
        landed(first_in.at[n], r_part[n]["one"])
        gr[rows(base1(n), 256), :] = fold(gr, base1(n), 256, first_in.at[n], 3)
        for d in (2, 1, 3):
            at = rows(base1(n) + place(snd, d) * 64, 64)
            go(gr.at[at], second_in.at[n, d - 1], towards(snd, d), 5 + n, r_part[n]["two"], 64)

    z_order = (4, 3, 5, 2, 6, 1, 7)

    def three(n):
        landed(second_in.at[n], r_part[n]["two"])
        gr[rows(base2(n), 64), :] = fold(gr, base2(n), 64, second_in.at[n], 3)
        for d in z_order:
            at = rows(base2(n) + ((z + d) % 8) * 8, 8)
            go(gr.at[at], third_in.at[n, d - 1], peer(dz=d), 5 + n, r_part[n]["three"], 8)

    def share(at, to, n, key, size):
        go(out_r.at[at, mine], out_r.at[at, mine], to, 9 + n, r_part[n][key], size)

    def back_z(n):
        landed(third_in.at[n], r_part[n]["three"])
        at = rows(base3(n), 8)
        out_r[at, mine] = fold(gr, base3(n), 8, third_in.at[n], 7)
        for d in z_order:
            share(at, peer(dz=d), n, "z", 8)

    def first_axis(n, at):
        for d in (2, 1, 3):
            share(at, towards(parts[n][1], d), n, f"f{d}", 64)

    def back_second(n):
        landed(out_r.at[0:56, mine], r_part[n]["z"])
        at = rows(base2(n), 64)
        first_axis(n, at)
        for d in (2, 1, 3):
            share(at, towards(parts[n][2], d), n, f"s{d}", 64)

    def back_first(n):
        for d in (1, 3, 2):
            at = rows(base1(n) + place(parts[n][2], -d) * 64, 64)
            landed(out_r.at[at, mine], r_part[n][f"s{d}"])
            first_axis(n, at)

    def to_pair(at):
        go(out_r.at[at, mine], out_r.at[at, mine], peer(dc=1), 13, r_pair, 256)

    def back_pair(n, d):
        p, fst, snd = parts[n]
        at = rows(p * 1024 + place(fst, -d) * 256, 256)
        if d:
            landed(out_r.at[at, mine], r_part[n][f"f{d}"])
        to_pair(at)

    for d in order:
        one(0, d)
        one(1, d)
    for d in order:
        one(2, d)
        one(3, d)

    ru = x * 128
    landed(u1, r_ux)
    gu[rows(ru, 128), :] = fold(gu, ru, 128, u1, 3)
    r_uz = slot()
    for d in (2, 1, 3):
        go(gu.at[rows(ru + ((zh + d) % 4) * 32, 32)], u2.at[d - 1], peer(dz=2 * d), 14, r_uz, 64)
    rq = y * 256
    landed(q1, r_qy)
    gq[rows(rq, 256), :] = fold(gq, rq, 256, q1, 3)
    r_qz = slot()
    go(gq.at[rows(rq + (1 - zl) * 128, 128)], q2.at[0], peer(dz=1 - 2 * zl), 15, r_qz, 128)

    two(0)
    two(1)
    ru2 = ru + zh * 32
    landed(u2, r_uz)
    out_u[rows(ru2, 32), :] = fold(gu, ru2, 32, u2, 3)
    r_ubz = slot()
    for d in (2, 1, 3):
        at = rows(ru2, 32)
        go(out_u.at[at], out_u.at[at], peer(dz=2 * d), 14, r_ubz, 64)
    rq2 = rq + zl * 128
    landed(q2, r_qz)
    out_q[rows(rq2, 128), mine] = fold(gq, rq2, 128, q2, 1)
    r_qbz = slot()
    at = rows(rq2, 128)
    go(out_q.at[at, mine], out_q.at[at, mine], peer(dz=1 - 2 * zl), 15, r_qbz, 128)
    three(0)
    three(1)
    two(2)
    two(3)
    landed(out_q.at[rows(rq + (1 - zl) * 128, 128), mine], r_qbz)
    r_qby, r_qc = slot(), slot()
    at = rows(rq, 256)
    for d in (2, 1, 3):
        go(out_q.at[at, mine], out_q.at[at, mine], peer(dy=d), 15, r_qby, 256)
    go(out_q.at[at, mine], out_q.at[at, mine], peer(dc=1), 15, r_qc, 256)
    landed(out_u.at[0:96], r_ubz)
    r_ubx = slot()
    for d in (2, 1, 3):
        at = rows(ru, 128)
        go(out_u.at[at], out_u.at[at], peer(dx=d), 14, r_ubx, 256)
    back_z(0)
    back_z(1)
    three(2)
    three(3)
    back_second(0)
    back_second(1)
    back_z(2)
    back_z(3)
    back_first(0)
    back_first(1)
    back_pair(0, 0)
    back_pair(1, 0)
    back_second(2)
    back_second(3)
    landed(out_q.at[0:768, mine], r_qby)
    for d in (1, 3, 2):
        at = rows(place("y", -d) * 256, 256)
        go(out_q.at[at, mine], out_q.at[at, mine], peer(dc=1), 15, r_qc, 256)
    back_first(2)
    back_first(3)
    back_pair(2, 0)
    back_pair(3, 0)
    for n in (0, 2):
        for d in (1, 3, 2):
            back_pair(n, d)
            back_pair(n + 1, d)
    landed(out_u.at[0:384], r_ubx)
    landed(out_q.at[:, others], r_qc)
    landed(out_r.at[:, others], r_pair)
    left(stat_in, 0)
    left(idx, 1)
    for s in sorted(sent):
        if s > 1:
            left(gr.at[0 : sent[s]], s)


SENDS = 16
RECVS = 56


def per_device(user_states, quot_rows, rem_table, neg_rem, pos_quot, pos_rem):
    vmem = pl.BlockSpec(memory_space=pltpu.VMEM)
    hbm = pl.BlockSpec(memory_space=pltpu.HBM)
    return pl.pallas_call(
        kernel,
        out_shape=(
            pltpu.VMEM((NU, D), F32),
            pltpu.VMEM((NN, D), F32),
            pltpu.VMEM((NR, D), F32),
        ),
        in_specs=[hbm] * 6,
        out_specs=(vmem, vmem, vmem),
        scratch_shapes=[
            pltpu.VMEM((NU, D), BF16),
            pltpu.VMEM((NN, D), BF16),
            pltpu.VMEM((NR, D), BF16),
            pltpu.VMEM((1, NN), jnp.int32),
            pltpu.VMEM((1, NU), jnp.int32),
            pltpu.VMEM((1, NU), jnp.int32),
            pltpu.VMEM((NN, D), F32),
            pltpu.VMEM((NN, D), BF16),
            pltpu.VMEM((NU, D), F32),
            pltpu.VMEM((NU, D), F32),
            pltpu.VMEM((NU, D), F32),
            pltpu.VMEM((NN, NU), F32),
            pltpu.VMEM((NN, NU), BF16),
            pltpu.VMEM((12, 128), F32),
            pltpu.VMEM((15, 12, 128), F32),
            pltpu.VMEM((2, NU), F32),
            pltpu.VMEM((2, NU), F32),
            pltpu.VMEM((2, NN + 2 * NU, H), F32),
            pltpu.VMEM((NN + 2 * NU, H), F32),
            pltpu.VMEM((NN + 2 * NU, D), BF16),
            pltpu.VMEM((2 * NU, D), BF16),
            pltpu.VMEM((NR, H), F32),
            pltpu.VMEM((NN, H), F32),
            pltpu.VMEM((NU, D), F32),
            pltpu.VMEM((4, 3, 256, H), F32),
            pltpu.VMEM((4, 3, 64, H), F32),
            pltpu.VMEM((4, 7, 8, H), F32),
            pltpu.VMEM((3, 256, H), F32),
            pltpu.VMEM((1, 128, H), F32),
            pltpu.VMEM((3, 128, D), F32),
            pltpu.VMEM((3, 32, D), F32),
            pltpu.SemaphoreType.DMA((6,)),
            pltpu.SemaphoreType.DMA((SENDS,)),
            pltpu.SemaphoreType.DMA((RECVS,)),
        ],
        compiler_params=pltpu.CompilerParams(
            collective_id=0, has_side_effects=True, vmem_limit_bytes=58 << 20
        ),
        cost_estimate=pl.CostEstimate(flops=12 << 30, bytes_accessed=9 << 20, transcendentals=1 << 20),
        name="sampled_softmax_grads",
    )(
        user_states, quot_rows, rem_table,
        neg_rem.reshape(1, NN), pos_quot.reshape(1, NU), pos_rem.reshape(1, NU),
    )


def solution(mesh):
    in_specs = (P("user", None), P("item", None), P(), P("item"), P("user"), P("user"))
    out_specs = (P("user", None), P("item", None), P())
    return jax.shard_map(
        per_device, mesh=mesh, in_specs=in_specs, out_specs=out_specs, check_vma=False
    )
```

time: 101 us -> 81.1 us (0.80)
  local copies, waits for them, and re-layouts: 14.9 us -> 3.78 us
  Pallas kernels: 85.3 us -> 76.6 us
    pallas_call x1, Pallas kernels: 85.3 us -> 76.6 us  [per_device(): pl.pallas_call(kernel, out_shape=(pltpu.VMEM((NU, D), F32), pltpu.VMEM((N...]
    transpose x2 -> x0, local copies, waits for them, and re-layouts: 7.16 us -> none  [the longest x1 5.6 us: per_device(): grad_rem = jnp.swapaxes(out_r, 0, 1).reshape(NR, D)]
    unnamed x5 -> x3, local copies, waits for them, and re-layouts: 7.75 us -> 3.78 us
where the time goes in v2:
time: 81.1 us; the launch traced here: 81 us
  Pallas kernels  76.6 us (94%)
  local copies, waits for them, and re-layouts  3.78 us (5%)
    pallas_call x1, Pallas kernels, per_device(): pl.pallas_call(kernel, out_shape=(pltpu.VMEM((NU, D), F32), pltpu.VMEM((N...  76.6 us
    unnamed x3, local copies, waits for them, and re-layouts  3.78 us

profile of v2, /device:TPU:1, one launch (start us, length us, event | category | flops | bytes accessed | tf_op | source)
XLA Modules:
  0.0 81.0 jit_solution(7325542354258660223)
XLA Ops:
  0.6 76.6 %sampled_softmax_grads.1 = (f32[512,256]{1,0:T(8,128)S(1)}, f32[1024,256]{1,0:T(8,128)S(1)}, f32[4096,256]{1,0:T(8,128)S(1)}) custom-call(bf16[512,256]{1,0:T(8,128)(2,1)} %user_hbm.1, bf16[1024,256]{1,0:T(8,128)(2,1)} %quot_hbm.1, bf16[4096,256]{1,0:T(8,128)(2,1)} %rem_hbm.1, s32[1,1024]{1,0:T(1,128)} %bitcast.3, s32[1,512]{1,0:T(1,128)} %bitcast.4, ...), custom_call_target="tpu_custom_call" | custom-call | flops 12884901888 | bytes 9437184 | tf_op jit(solution)/shard_map/sampled_softmax_grads/pallas_call | solution.py:444
  77.2 0.8 copy.12
  78.0 1.0 %copy.13 = f32[1024,256]{1,0:T(8,128)} copy(f32[1024,256]{1,0:T(8,128)S(1)} %get-tuple-element.4) | data formatting | bytes 2097152
  79.0 2.0 %copy.14 = f32[4096,256]{1,0:T(8,128)} copy(f32[4096,256]{1,0:T(8,128)S(1)} %get-tuple-element.5) | data formatting | bytes 8388608

commit v3 on v2

--- a/solution.py
+++ b/solution.py
@@ -42,8 +42,8 @@
     user_hbm, quot_hbm, rem_hbm, neg_rem_hbm, pos_quot_hbm, pos_rem_hbm,
     out_u, out_q, out_r,
     user, quot, rem, neg_rem, pos_quot, pos_rem,
-    remneg, emb, rempos, qpos, pemb, st, pt, stat, stat_in, idx, idx_in, half, half_in,
-    rhs, rhsq, gr, gq, gu, first_in, second_in, third_in, q1, q2, u1, u2,
+    remneg, emb, posq, posq_in, pemb, st, pt, stat, stat_in, idx, idx_in, scales, scales_in,
+    half, half_in, rhs, rhsq, gr, gq, gu, mid, first_in, second_in, third_in, q1, q2, u1, u2,
     load, send, recv,
 ):
     x, y, z, c = coords()
@@ -128,9 +128,18 @@
         r0 = pl.multiple_of(b * 256, 256)
         got_r = jnp.dot(picks(pos_rem, r0, 0, lanes_r), rem[...], preferred_element_type=F32)
         got_q = jnp.dot(picks(pos_quot, r0, first, lanes_q), quot[...], preferred_element_type=F32)
-        rempos[pl.ds(r0, 256), :] = got_r
-        qpos[pl.ds(r0, 256), :] = got_q
         pemb[pl.ds(r0, 256), :] = (got_q * got_r).astype(BF16).astype(F32)
+        own = []
+        for k in range(2):
+            at = pl.ds(pl.multiple_of(r0 + k * 128, 128), 128)
+            col = columns_of((pos_quot[0:1, at] - first).astype(F32))
+            own.append((col >= 0.0) & (col < float(NN)))
+        own = jnp.concatenate(own, axis=0)
+        for h in range(2):
+            cols = slice(h * H, (h + 1) * H)
+            mask = jnp.where(own, user[pl.ds(r0, 256), cols].astype(F32), 0.0)
+            posq[h, 0, pl.ds(r0, 256), :] = mask * got_q[:, cols]
+            posq[h, 1, pl.ds(r0, 256), :] = mask * got_r[:, cols]
         return carry
 
     for n in (3, 4, 5):
@@ -138,6 +147,11 @@
     lax.fori_loop(0, NU // 256, gather_pos, 0)
     idx[0:1, :] = pos_rem[...].astype(F32)
     idx[1:2, :] = (pos_quot[...] - first).astype(F32)
+
+    pl.semaphore_wait(barrier, len(peers))
+    r_stat, r_idx, r_half, r_pos, r_coef, r_ux = (slot() for _ in range(6))
+    go(idx, idx_in, peer(dc=1), 1, r_idx, 8)
+    go(posq.at[1 - c], posq_in, peer(dc=1), 2, r_pos, 2 * NU)
 
     def scores(b, top):
         r0 = pl.multiple_of(b * 256, 256)
@@ -153,6 +167,7 @@
     def totals(b, tot):
         r0 = pl.multiple_of(b * 256, 256)
         e = jnp.exp(st[pl.ds(r0, 256), :] - top_row)
+        pt[pl.ds(r0, 256), :] = e.astype(BF16)
         return tot + jnp.sum(e.reshape(32, 8, NU), axis=0)
 
     tot8 = lax.fori_loop(0, NN // 256, totals, jnp.zeros((8, NU), F32))
@@ -165,11 +180,24 @@
         prod = prod[:, :H] + prod[:, H:]
         stat[8 + k : 9 + k, :] = SCALE * jnp.sum(jnp.transpose(prod), axis=0, keepdims=True)
 
-    pl.semaphore_wait(barrier, len(peers))
-    r_stat, r_idx, r_half = slot(), slot(), slot()
     for n, p in enumerate(item_peers):
         go(stat, stat_in.at[n], peer(*p), 0, r_stat, 12)
-    go(idx, idx_in, peer(dc=1), 1, r_idx, 8)
+
+    def users(b, carry):
+        at = pl.ds(pl.multiple_of(b * 256, 256), 256)
+        g = lax.dot_general(
+            pt[at, :], emb[at, :], (((0,), (0,)), ((), ())), preferred_element_type=F32
+        )
+        gu[...] += g
+        return carry
+
+    gu[...] = jnp.zeros_like(gu)
+    lax.fori_loop(0, NN // 256, users, 0)
+    for d in (1, 3, 2):
+        at = rows(((x + d) % 4) * 128, 128)
+        go(gu.at[at], u1.at[d - 1], peer(dx=d), 3, r_ux, 256)
+        go(pemb.at[at], u1.at[2 + d], peer(dx=d), 3, r_ux, 256)
+
     landed(stat_in, r_stat)
     tops = [stat[0:4, :]] + [stat_in[n, 0:4, :] for n in range(15)]
     top_neg = functools.reduce(jnp.maximum, tops)
@@ -181,80 +209,74 @@
     top = jnp.maximum(top_neg, pos_score)
     lse = top + jnp.log(total * jnp.exp(top_neg - top) + jnp.exp(pos_score - top))
     coef = SCALE * (jnp.exp(pos_score - lse) - 1.0)
+    scales[0:4, :] = lse
+    scales[4:8, :] = coef
     lse_row = jnp.concatenate([lse[k : k + 1, :] for k in range(4)], axis=1)
+
+    go(scales, scales_in, peer(dc=1), 1, r_coef, 8)
 
     def backward(b, carry):
         r0 = pl.multiple_of(b * 256, 256)
         at = pl.ds(r0, 256)
         p = jnp.exp(st[at, :] - lse_row).astype(BF16)
-        pt[at, :] = p
         g = SCALE * jnp.dot(p, user[...], preferred_element_type=F32)
         half[0, at, :] = g[:, :H]
         half[1, at, :] = g[:, H:]
         return carry
 
-    lax.fori_loop(0, NN // 256, backward, 0)
-    for k in range(4):
-        at = slice(k * 128, (k + 1) * 128)
-        col = columns_of(coef[k : k + 1, :])
-        slot_col = columns_of(idx[1:2, at])
-        owned = (slot_col >= 0.0) & (slot_col < float(NN))
-        for h in range(2):
-            cols = slice(h * H, (h + 1) * H)
-            gp = jnp.where(owned, col * user[at, cols].astype(F32), 0.0)
-            half[h, NN + k * 128 : NN + (k + 1) * 128, :] = gp * qpos[at, cols]
-            half[h, NN + NU + k * 128 : NN + NU + (k + 1) * 128, :] = gp * rempos[at, cols]
-            gu[at, cols] = col * pemb[at, cols]
-    go(half.at[1 - c], half_in, peer(dc=1), 2, r_half, NN + 2 * NU)
-
-    def users(b, carry):
-        at = pl.ds(pl.multiple_of(b * 256, 256), 256)
-        g = lax.dot_general(
-            pt[at, :], emb[at, :], (((0,), (0,)), ((), ())), preferred_element_type=F32
-        )
-        gu[...] += SCALE * g
-        return carry
-
-    lax.fori_loop(0, NN // 256, users, 0)
-    r_ux = slot()
-    for d in (1, 3, 2):
-        go(gu.at[rows(((x + d) % 4) * 128, 128)], u1.at[d - 1], peer(dx=d), 3, r_ux, 256)
+    for k in range(2):
+        lax.fori_loop(2 * k, 2 * k + 2, backward, 0)
+        at = pl.ds(k * 512, 512)
+        go(half.at[1 - c, at], half_in.at[at], peer(dc=1), 2, r_half, 512)
 
     landed(idx_in, r_idx)
+    landed(posq_in, r_pos)
+
+    def scaled(base, src, coefs):
+        for k in range(4):
+            col = columns_of(coefs[k : k + 1, :])
+            at = slice(k * 128, (k + 1) * 128)
+            to = slice(base + k * 128, base + (k + 1) * 128)
+            hi, lo = split_pair(col * src[0, at, :])
+            rhs[NN + to.start : NN + to.stop, :H] = hi
+            rhs[NN + to.start : NN + to.stop, H:] = lo
+            hi, lo = split_pair(col * src[1, at, :])
+            rhsq[to, :H] = hi
+            rhsq[to, H:] = lo
+
+    scaled(0, posq.at[c], coef)
+    landed(scales_in, r_coef)
+    scaled(NU, posq_in, scales_in[4:8, :])
+
+    slots = jnp.concatenate([idx[1:2, :], idx_in[1:2, :]], axis=1)
+    down_q = lax.broadcasted_iota(jnp.int32, (256, 2 * NU), 0).astype(F32)
+    for b in range(NN // 256):
+        pick = jnp.where(down_q + float(b * 256) == slots, 1.0, 0.0).astype(BF16)
+        g = jnp.dot(pick, rhsq[...], preferred_element_type=F32)
+        gq[b * 256 : (b + 1) * 256, :] = g[:, :H] + g[:, H:]
+
     landed(half_in, r_half)
     first_half = c == 0
 
-    def pair(b, carry):
-        at = pl.ds(pl.multiple_of(b * 256, 256), 256)
-        g = half[c, at, :] + half_in[at, :]
-        q = jnp.where(first_half, quot[at, :H].astype(F32), quot[at, H:].astype(F32))
-        hi, lo = split_pair(g * q)
-        rhs[at, :H] = hi
-        rhs[at, H:] = lo
-        rn = jnp.where(first_half, remneg[at, :H], remneg[at, H:])
-        gq[at, :] = g * rn
-        return carry
-
-    lax.fori_loop(0, NN // 256, pair, 0)
-    for base, src in ((0, half.at[c]), (NU, half_in)):
-        hi, lo = split_pair(src[NN : NN + NU, :])
-        rhs[NN + base : NN + base + NU, :H] = hi
-        rhs[NN + base : NN + base + NU, H:] = lo
-        hi, lo = split_pair(src[NN + NU : NN + 2 * NU, :])
-        rhsq[base : base + NU, :H] = hi
-        rhsq[base : base + NU, H:] = lo
-
-    slots = jnp.concatenate([idx[1:2, :], idx_in[1:2, :]], axis=1)
-    down_q = lax.broadcasted_iota(jnp.int32, (256, 2 * NU), 0).astype(F32)
-    r_qy = slot()
-    for d in (2, 1, 3, 0):
-        r0 = ((y + d) % 4) * 256
-        at = rows(r0, 256)
-        pick = jnp.where(down_q + lax.convert_element_type(r0, F32) == slots, 1.0, 0.0).astype(BF16)
-        g = jnp.dot(pick, rhsq[...], preferred_element_type=F32)
-        gq[at, :] += g[:, :H] + g[:, H:]
-        if d:
-            go(gq.at[at], q1.at[d - 1], peer(dy=d), 4, r_qy, 256)
+    def pair(first_row):
+        def step(b, carry):
+            at = rows(first_row + b * 256, 256)
+            g = half[c, at, :] + half_in[at, :]
+            q = jnp.where(first_half, quot[at, :H].astype(F32), quot[at, H:].astype(F32))
+            hi, lo = split_pair(g * q)
+            rhs[at, :H] = hi
+            rhs[at, H:] = lo
+            rn = jnp.where(first_half, remneg[at, :H], remneg[at, H:])
+            gq[at, :] += g * rn
+            return carry
+
+        lax.fori_loop(0, 2, step, 0)
+
+    r_qz = slot()
+    pair((1 - zl) * 512)
+    go(gq.at[rows((1 - zl) * 512, 512)], q1.at[0], peer(dz=1 - 2 * zl), 4, r_qz, 512)
+    rq = zl * 512
+    pair(rq)
 
     which = jnp.concatenate([neg_rem[...].astype(F32), idx[0:1, :], idx_in[0:1, :]], axis=1)
     down_r = lax.broadcasted_iota(jnp.int32, (256, NN + 2 * NU), 0).astype(F32)
@@ -352,56 +374,67 @@
     for d in order:
         one(0, d)
         one(1, d)
+    ru = x * 128
+    landed(u1, r_ux)
+    lse_mine = scales[pl.ds(x, 1), :]
+    at = rows(ru, 128)
+    total_u = jnp.zeros((128, D), F32)
+    pos_u = jnp.zeros((128, D), F32)
+    for d in range(4):
+        top_d = stat_in[d - 1, pl.ds(x, 1), :] if d else stat[pl.ds(x, 1), :]
+        col = columns_of(SCALE * jnp.exp(top_d - lse_mine))
+        col = jnp.concatenate([col, col], axis=1)
+        total_u = total_u + col * (u1[d - 1] if d else gu[at, :])
+        pos_u = pos_u + (u1[2 + d] if d else pemb[at, :])
+    col = columns_of(scales[pl.ds(4 + x, 1), :])
+    mid[...] = total_u + jnp.concatenate([col, col], axis=1) * pos_u
+    r_uz = slot()
+    for d in (2, 1, 3):
+        go(mid.at[rows(((zh + d) % 4) * 32, 32)], u2.at[d - 1], peer(dz=2 * d), 14, r_uz, 64)
     for d in order:
         one(2, d)
         one(3, d)
-
-    ru = x * 128
-    landed(u1, r_ux)
-    gu[rows(ru, 128), :] = fold(gu, ru, 128, u1, 3)
-    r_uz = slot()
+    landed(q1, r_qz)
+    gq[rows(rq, 512), :] = fold(gq, rq, 512, q1, 1)
+    r_qy = slot()
     for d in (2, 1, 3):
-        go(gu.at[rows(ru + ((zh + d) % 4) * 32, 32)], u2.at[d - 1], peer(dz=2 * d), 14, r_uz, 64)
-    rq = y * 256
-    landed(q1, r_qy)
-    gq[rows(rq, 256), :] = fold(gq, rq, 256, q1, 3)
-    r_qz = slot()
-    go(gq.at[rows(rq + (1 - zl) * 128, 128)], q2.at[0], peer(dz=1 - 2 * zl), 15, r_qz, 128)
+        at = rows(rq + place("y", d) * 128, 128)
+        go(gq.at[at], q2.at[d - 1], peer(dy=d), 15, r_qy, 128)
 
     two(0)
     two(1)
     ru2 = ru + zh * 32
     landed(u2, r_uz)
-    out_u[rows(ru2, 32), :] = fold(gu, ru2, 32, u2, 3)
+    out_u[rows(ru2, 32), :] = fold(mid, zh * 32, 32, u2, 3)
     r_ubz = slot()
     for d in (2, 1, 3):
         at = rows(ru2, 32)
         go(out_u.at[at], out_u.at[at], peer(dz=2 * d), 14, r_ubz, 64)
-    rq2 = rq + zl * 128
-    landed(q2, r_qz)
-    out_q[rows(rq2, 128), mine] = fold(gq, rq2, 128, q2, 1)
-    r_qbz = slot()
-    at = rows(rq2, 128)
-    go(out_q.at[at, mine], out_q.at[at, mine], peer(dz=1 - 2 * zl), 15, r_qbz, 128)
     three(0)
     three(1)
+    rq2 = rq + y * 128
+    landed(q2, r_qy)
+    out_q[rows(rq2, 128), mine] = fold(gq, rq2, 128, q2, 3)
+    r_qby = slot()
+    at = rows(rq2, 128)
+    for d in (2, 1, 3):
+        go(out_q.at[at, mine], out_q.at[at, mine], peer(dy=d), 15, r_qby, 128)
     two(2)
     two(3)
-    landed(out_q.at[rows(rq + (1 - zl) * 128, 128), mine], r_qbz)
-    r_qby, r_qc = slot(), slot()
-    at = rows(rq, 256)
-    for d in (2, 1, 3):
-        go(out_q.at[at, mine], out_q.at[at, mine], peer(dy=d), 15, r_qby, 256)
-    go(out_q.at[at, mine], out_q.at[at, mine], peer(dc=1), 15, r_qc, 256)
+    back_z(0)
+    back_z(1)
     landed(out_u.at[0:96], r_ubz)
     r_ubx = slot()
     for d in (2, 1, 3):
         at = rows(ru, 128)
         go(out_u.at[at], out_u.at[at], peer(dx=d), 14, r_ubx, 256)
-    back_z(0)
-    back_z(1)
     three(2)
     three(3)
+    landed(out_q.at[0:384, mine], r_qby)
+    r_qbz, r_qc = slot(), slot()
+    at = rows(rq, 512)
+    go(out_q.at[at, mine], out_q.at[at, mine], peer(dz=1 - 2 * zl), 15, r_qbz, 512)
+    go(out_q.at[at, mine], out_q.at[at, mine], peer(dc=1), 15, r_qc, 512)
     back_second(0)
     back_second(1)
     back_z(2)
@@ -412,10 +445,9 @@
     back_pair(1, 0)
     back_second(2)
     back_second(3)
-    landed(out_q.at[0:768, mine], r_qby)
-    for d in (1, 3, 2):
-        at = rows(place("y", -d) * 256, 256)
-        go(out_q.at[at, mine], out_q.at[at, mine], peer(dc=1), 15, r_qc, 256)
+    at = rows((1 - zl) * 512, 512)
+    landed(out_q.at[at, mine], r_qbz)
+    go(out_q.at[at, mine], out_q.at[at, mine], peer(dc=1), 15, r_qc, 512)
     back_first(2)
     back_first(3)
     back_pair(2, 0)
@@ -428,9 +460,8 @@
     landed(out_q.at[:, others], r_qc)
     landed(out_r.at[:, others], r_pair)
     left(stat_in, 0)
-    left(idx, 1)
     for s in sorted(sent):
-        if s > 1:
+        if s > 0:
             left(gr.at[0 : sent[s]], s)
 
 
@@ -459,8 +490,8 @@
             pltpu.VMEM((1, NU), jnp.int32),
             pltpu.VMEM((NN, D), F32),
             pltpu.VMEM((NN, D), BF16),
-            pltpu.VMEM((NU, D), F32),
-            pltpu.VMEM((NU, D), F32),
+            pltpu.VMEM((2, 2, NU, H), F32),
+            pltpu.VMEM((2, NU, H), F32),
             pltpu.VMEM((NU, D), F32),
             pltpu.VMEM((NN, NU), F32),
             pltpu.VMEM((NN, NU), BF16),
@@ -468,19 +499,22 @@
             pltpu.VMEM((15, 12, 128), F32),
             pltpu.VMEM((2, NU), F32),
             pltpu.VMEM((2, NU), F32),
-            pltpu.VMEM((2, NN + 2 * NU, H), F32),
-            pltpu.VMEM((NN + 2 * NU, H), F32),
+            pltpu.VMEM((8, 128), F32),
+            pltpu.VMEM((8, 128), F32),
+            pltpu.VMEM((2, NN, H), F32),
+            pltpu.VMEM((NN, H), F32),
             pltpu.VMEM((NN + 2 * NU, D), BF16),
             pltpu.VMEM((2 * NU, D), BF16),
             pltpu.VMEM((NR, H), F32),
             pltpu.VMEM((NN, H), F32),
             pltpu.VMEM((NU, D), F32),
+            pltpu.VMEM((128, D), F32),
             pltpu.VMEM((4, 3, 256, H), F32),
             pltpu.VMEM((4, 3, 64, H), F32),
             pltpu.VMEM((4, 7, 8, H), F32),
-            pltpu.VMEM((3, 256, H), F32),
-            pltpu.VMEM((1, 128, H), F32),
-            pltpu.VMEM((3, 128, D), F32),
+            pltpu.VMEM((1, 512, H), F32),
+            pltpu.VMEM((3, 128, H), F32),
+            pltpu.VMEM((6, 128, D), F32),
             pltpu.VMEM((3, 32, D), F32),
             pltpu.SemaphoreType.DMA((6,)),
             pltpu.SemaphoreType.DMA((SENDS,)),

time: 81.1 us -> 80 us (0.986)
  Pallas kernels: 76.6 us -> 75.4 us
    pallas_call x1, Pallas kernels: 76.6 us -> 75.4 us  [per_device(): pl.pallas_call(kernel, out_shape=(pltpu.VMEM((NU, D), F32), pltpu.VMEM((N...]
where the time goes in v3:
time: 80 us; the launch traced here: 79.8 us
  Pallas kernels  75.4 us (94%)
  local copies, waits for them, and re-layouts  3.78 us (5%)
    pallas_call x1, Pallas kernels, per_device(): pl.pallas_call(kernel, out_shape=(pltpu.VMEM((NU, D), F32), pltpu.VMEM((N...  75.4 us
    unnamed x3, local copies, waits for them, and re-layouts  3.78 us

profile of v3, /device:TPU:1, one launch (start us, length us, event | category | flops | bytes accessed | tf_op | source)
XLA Modules:
  0.0 79.8 jit_solution(11367640002746422992)
XLA Ops:
  0.6 75.4 %sampled_softmax_grads.1 = (f32[512,256]{1,0:T(8,128)S(1)}, f32[1024,256]{1,0:T(8,128)S(1)}, f32[4096,256]{1,0:T(8,128)S(1)}) custom-call(bf16[512,256]{1,0:T(8,128)(2,1)} %user_hbm.1, bf16[1024,256]{1,0:T(8,128)(2,1)} %quot_hbm.1, bf16[4096,256]{1,0:T(8,128)(2,1)} %rem_hbm.1, s32[1,1024]{1,0:T(1,128)} %bitcast.3, s32[1,512]{1,0:T(1,128)} %bitcast.4, ...), custom_call_target="tpu_custom_call" | custom-call | flops 12884901888 | bytes 9437184 | tf_op jit(solution)/shard_map/sampled_softmax_grads/pallas_call | solution.py:475
  76.1 0.8 copy.12
  76.9 1.0 %copy.13 = f32[1024,256]{1,0:T(8,128)} copy(f32[1024,256]{1,0:T(8,128)S(1)} %get-tuple-element.4) | data formatting | bytes 2097152
  77.8 2.0 %copy.14 = f32[4096,256]{1,0:T(8,128)} copy(f32[4096,256]{1,0:T(8,128)S(1)} %get-tuple-element.5) | data formatting | bytes 8388608

commit v4 on v3

--- a/solution.py
+++ b/solution.py
@@ -43,7 +43,7 @@
     out_u, out_q, out_r,
     user, quot, rem, neg_rem, pos_quot, pos_rem,
     remneg, emb, posq, posq_in, pemb, st, pt, stat, stat_in, idx, idx_in, scales, scales_in,
-    half, half_in, rhs, rhsq, gr, gq, gu, mid, first_in, second_in, third_in, q1, q2, u1, u2,
+    half, half_in, low_hot, rhs, rhsq, gr, gq, gu, mid, first_in, second_in, third_in, q1, q2, u1, u2,
     load, send, recv,
 ):
     x, y, z, c = coords()
@@ -100,21 +100,25 @@
     def rows(first_row, count):
         return pl.ds(pl.multiple_of(first_row, 8), count)
 
-    lanes_r = lax.broadcasted_iota(jnp.int32, (256, NR), 1).astype(F32)
-    lanes_q = lax.broadcasted_iota(jnp.int32, (256, NN), 1).astype(F32)
-
-    def picks(row_ref, first, shift, lanes):
-        parts = []
+    lane = lax.broadcasted_iota(jnp.int32, (128, 128), 1)
+
+    def picks(row_ref, first, shift, width):
+        lows, highs = [], []
         for k in range(2):
             at = pl.ds(pl.multiple_of(first + k * 128, 128), 128)
-            parts.append(columns_of((row_ref[0:1, at] - shift).astype(F32)))
-        col = jnp.concatenate(parts, axis=0)
-        wide = jnp.concatenate([col] * (lanes.shape[1] // 128), axis=1)
-        return jnp.where(wide == lanes, 1.0, 0.0).astype(BF16)
+            value = row_ref[0:1, at] - shift
+            low = columns_of((value & 127).astype(F32))
+            lows.append(jnp.where(low == lane.astype(F32), 1.0, 0.0).astype(BF16))
+            highs.append(columns_of((value >> 7).astype(F32)).astype(BF16))
+        low, high = jnp.concatenate(lows, axis=0), jnp.concatenate(highs, axis=0)
+        zero = jnp.zeros_like(low)
+        return jnp.concatenate(
+            [jnp.where(high == jnp.full_like(high, k), low, zero) for k in range(width // 128)], axis=1
+        )
 
     def gather_neg(b, carry):
         r0 = pl.multiple_of(b * 256, 256)
-        got = jnp.dot(picks(neg_rem, r0, 0, lanes_r), rem[...], preferred_element_type=F32)
+        got = jnp.dot(picks(neg_rem, r0, 0, NR), rem[...], preferred_element_type=F32)
         remneg[pl.ds(r0, 256), :] = got
         emb[pl.ds(r0, 256), :] = (quot[pl.ds(r0, 256), :].astype(F32) * got).astype(BF16)
         return carry
@@ -126,8 +130,8 @@
 
     def gather_pos(b, carry):
         r0 = pl.multiple_of(b * 256, 256)
-        got_r = jnp.dot(picks(pos_rem, r0, 0, lanes_r), rem[...], preferred_element_type=F32)
-        got_q = jnp.dot(picks(pos_quot, r0, first, lanes_q), quot[...], preferred_element_type=F32)
+        got_r = jnp.dot(picks(pos_rem, r0, 0, NR), rem[...], preferred_element_type=F32)
+        got_q = jnp.dot(picks(pos_quot, r0, first, NN), quot[...], preferred_element_type=F32)
         pemb[pl.ds(r0, 256), :] = (got_q * got_r).astype(BF16).astype(F32)
         own = []
         for k in range(2):
@@ -197,6 +201,14 @@
         at = rows(((x + d) % 4) * 128, 128)
         go(gu.at[at], u1.at[d - 1], peer(dx=d), 3, r_ux, 256)
         go(pemb.at[at], u1.at[2 + d], peer(dx=d), 3, r_ux, 256)
+
+    landed(idx_in, r_idx)
+    which = jnp.concatenate([neg_rem[...].astype(F32), idx[0:1, :], idx_in[0:1, :]], axis=1)
+    high = jnp.floor(which * (1.0 / 256.0))
+    low = which - 256.0 * high
+    for b in range(2):
+        down = lax.broadcasted_iota(jnp.int32, (128, NN + 2 * NU), 0).astype(F32) + float(b * 128)
+        low_hot[b * 128 : (b + 1) * 128, :] = jnp.where(down == low, 1.0, 0.0).astype(BF16)
 
     landed(stat_in, r_stat)
     tops = [stat[0:4, :]] + [stat_in[n, 0:4, :] for n in range(15)]
@@ -229,7 +241,6 @@
         at = pl.ds(k * 512, 512)
         go(half.at[1 - c, at], half_in.at[at], peer(dc=1), 2, r_half, 512)
 
-    landed(idx_in, r_idx)
     landed(posq_in, r_pos)
 
     def scaled(base, src, coefs):
@@ -278,12 +289,10 @@
     rq = zl * 512
     pair(rq)
 
-    which = jnp.concatenate([neg_rem[...].astype(F32), idx[0:1, :], idx_in[0:1, :]], axis=1)
-    down_r = lax.broadcasted_iota(jnp.int32, (256, NN + 2 * NU), 0).astype(F32)
     axes = {"x": x, "y": y}
     order = (2, 1, 3, 0)
     parts = [(0, "x", "y"), (1, "y", "x"), (2, "x", "y"), (3, "y", "x")]
-    r_part = [{k: slot() for k in ("one", "two", "three", "z", "s1", "s2", "s3", "f1", "f2", "f3")} for _ in parts]
+    r_part = [{k: slot() for k in KINDS} for _ in parts]
     r_pair = slot()
 
     def towards(axis, d):
@@ -292,14 +301,37 @@
     def place(axis, d=0):
         return (axes[axis] + d) % 4
 
-    def one(n, d):
+    def made(n, d):
         p, fst, snd = parts[n]
         r0 = p * 1024 + place(fst, d) * 256
-        pick = jnp.where(down_r == which - lax.convert_element_type(r0, F32), 1.0, 0.0).astype(BF16)
-        g = jnp.dot(pick, rhs[...], preferred_element_type=F32)
+        mask = jnp.where(high == lax.convert_element_type(r0 // 256, F32), 1.0, 0.0).astype(BF16)
+        g = jnp.dot(low_hot[...] * mask, rhs[...], preferred_element_type=F32)
         gr[rows(r0, 256), :] = g[:, :H] + g[:, H:]
+
+    def give(n, d):
+        p, fst, snd = parts[n]
+        r0 = p * 1024 + place(fst, d) * 256
+        up, down = rows(r0, 128), rows(r0 + 128, 128)
+        if d == 2:
+            go(gr.at[up], first_in.at[n, 2, 0:128], towards(fst, 1), 5 + n, r_part[n]["join"], 128)
+            go(gr.at[down], first_in.at[n, 2, 128:256], towards(fst, 3), 5 + n, r_part[n]["join"], 128)
+        elif d == 1:
+            go(gr.at[down], first_in.at[n, 0, 128:256], towards(fst, 1), 5 + n, r_part[n]["one"], 128)
+        else:
+            go(gr.at[up], first_in.at[n, 1, 0:128], towards(fst, 3), 5 + n, r_part[n]["one"], 128)
+
+    def join(n):
+        p, fst, snd = parts[n]
+        landed(first_in.at[n, 2], r_part[n]["join"])
+        for d, k, h in ((1, 0, 0), (3, 1, 128)):
+            at = rows(p * 1024 + place(fst, d) * 256 + h, 128)
+            gr[at, :] += first_in[n, 2, h : h + 128, :]
+            go(gr.at[at], first_in.at[n, k, h : h + 128], towards(fst, d), 5 + n, r_part[n]["one"], 128)
+
+    def one(n, d):
+        made(n, d)
         if d:
-            go(gr.at[rows(r0, 256)], first_in.at[n, d - 1], towards(fst, d), 5 + n, r_part[n]["one"], 256)
+            give(n, d)
 
     def fold(dst, r0, count, slots_ref, n):
         v = dst[rows(r0, count), :]
@@ -319,8 +351,8 @@
 
     def two(n):
         p, fst, snd = parts[n]
-        landed(first_in.at[n], r_part[n]["one"])
-        gr[rows(base1(n), 256), :] = fold(gr, base1(n), 256, first_in.at[n], 3)
+        landed(first_in.at[n, 0:2], r_part[n]["one"])
+        gr[rows(base1(n), 256), :] = fold(gr, base1(n), 256, first_in.at[n], 2)
         for d in (2, 1, 3):
             at = rows(base1(n) + place(snd, d) * 64, 64)
             go(gr.at[at], second_in.at[n, d - 1], towards(snd, d), 5 + n, r_part[n]["two"], 64)
@@ -344,14 +376,22 @@
         for d in z_order:
             share(at, peer(dz=d), n, "z", 8)
 
-    def first_axis(n, at):
-        for d in (2, 1, 3):
-            share(at, towards(parts[n][1], d), n, f"f{d}", 64)
+    def first_axis(n, k):
+        at = rows(base1(n) + place(parts[n][2], -k) * 64, 64)
+        for d in (1, 3):
+            share(at, towards(parts[n][1], d), n, f"f{d}_{k}", 64)
+
+    def pass_on(n, k):
+        p, fst, snd = parts[n]
+        for d, h in ((1, 0), (3, 32)):
+            r0 = p * 1024 + place(fst, -d) * 256 + place(snd, -k) * 64
+            landed(out_r.at[rows(r0, 64), mine], r_part[n][f"f{d}_{k}"])
+            share(rows(r0 + h, 32), towards(fst, d), n, f"h{d}", 32)
 
     def back_second(n):
         landed(out_r.at[0:56, mine], r_part[n]["z"])
         at = rows(base2(n), 64)
-        first_axis(n, at)
+        first_axis(n, 0)
         for d in (2, 1, 3):
             share(at, towards(parts[n][2], d), n, f"s{d}", 64)
 
@@ -359,7 +399,7 @@
         for d in (1, 3, 2):
             at = rows(base1(n) + place(parts[n][2], -d) * 64, 64)
             landed(out_r.at[at, mine], r_part[n][f"s{d}"])
-            first_axis(n, at)
+            first_axis(n, d)
 
     def to_pair(at):
         go(out_r.at[at, mine], out_r.at[at, mine], peer(dc=1), 13, r_pair, 256)
@@ -367,13 +407,16 @@
     def back_pair(n, d):
         p, fst, snd = parts[n]
         at = rows(p * 1024 + place(fst, -d) * 256, 256)
-        if d:
-            landed(out_r.at[at, mine], r_part[n][f"f{d}"])
+        if d == 2:
+            landed(out_r.at[0:128, mine], r_part[n]["h1"])
+            landed(out_r.at[0:128, mine], r_part[n]["h3"])
         to_pair(at)
 
     for d in order:
         one(0, d)
         one(1, d)
+    join(0)
+    join(1)
     ru = x * 128
     landed(u1, r_ux)
     lse_mine = scales[pl.ds(x, 1), :]
@@ -394,15 +437,20 @@
     for d in order:
         one(2, d)
         one(3, d)
+    join(2)
+    join(3)
+    two(0)
+    two(1)
+    two(2)
+    two(3)
     landed(q1, r_qz)
     gq[rows(rq, 512), :] = fold(gq, rq, 512, q1, 1)
     r_qy = slot()
     for d in (2, 1, 3):
         at = rows(rq + place("y", d) * 128, 128)
         go(gq.at[at], q2.at[d - 1], peer(dy=d), 15, r_qy, 128)
-
-    two(0)
-    two(1)
+    three(0)
+    three(1)
     ru2 = ru + zh * 32
     landed(u2, r_uz)
     out_u[rows(ru2, 32), :] = fold(mid, zh * 32, 32, u2, 3)
@@ -410,8 +458,8 @@
     for d in (2, 1, 3):
         at = rows(ru2, 32)
         go(out_u.at[at], out_u.at[at], peer(dz=2 * d), 14, r_ubz, 64)
-    three(0)
-    three(1)
+    three(2)
+    three(3)
     rq2 = rq + y * 128
     landed(q2, r_qy)
     out_q[rows(rq2, 128), mine] = fold(gq, rq2, 128, q2, 3)
@@ -419,17 +467,15 @@
     at = rows(rq2, 128)
     for d in (2, 1, 3):
         go(out_q.at[at, mine], out_q.at[at, mine], peer(dy=d), 15, r_qby, 128)
-    two(2)
-    two(3)
     back_z(0)
     back_z(1)
+    back_z(2)
+    back_z(3)
     landed(out_u.at[0:96], r_ubz)
-    r_ubx = slot()
-    for d in (2, 1, 3):
-        at = rows(ru, 128)
-        go(out_u.at[at], out_u.at[at], peer(dx=d), 14, r_ubx, 256)
-    three(2)
-    three(3)
+    r_ub1, r_ub3, r_uh = slot(), slot(), slot()
+    at = rows(ru, 128)
+    go(out_u.at[at], out_u.at[at], peer(dx=1), 14, r_ub1, 256)
+    go(out_u.at[at], out_u.at[at], peer(dx=3), 14, r_ub3, 256)
     landed(out_q.at[0:384, mine], r_qby)
     r_qbz, r_qc = slot(), slot()
     at = rows(rq, 512)
@@ -437,26 +483,41 @@
     go(out_q.at[at, mine], out_q.at[at, mine], peer(dc=1), 15, r_qc, 512)
     back_second(0)
     back_second(1)
-    back_z(2)
-    back_z(3)
+    back_second(2)
+    back_second(3)
+    pass_on(0, 0)
+    pass_on(1, 0)
+    pass_on(2, 0)
+    pass_on(3, 0)
+    for d, h, r in ((1, 0, r_ub1), (3, 64, r_ub3)):
+        r0 = ((x - d) % 4) * 128
+        landed(out_u.at[rows(r0, 128)], r)
+        at = rows(r0 + h, 64)
+        go(out_u.at[at], out_u.at[at], peer(dx=d), 14, r_uh, 128)
     back_first(0)
     back_first(1)
+    back_first(2)
+    back_first(3)
     back_pair(0, 0)
     back_pair(1, 0)
-    back_second(2)
-    back_second(3)
+    back_pair(2, 0)
+    back_pair(3, 0)
+    for k in (1, 3, 2):
+        pass_on(0, k)
+        pass_on(1, k)
+    for k in (1, 3, 2):
+        pass_on(2, k)
+        pass_on(3, k)
     at = rows((1 - zl) * 512, 512)
     landed(out_q.at[at, mine], r_qbz)
     go(out_q.at[at, mine], out_q.at[at, mine], peer(dc=1), 15, r_qc, 512)
-    back_first(2)
-    back_first(3)
-    back_pair(2, 0)
-    back_pair(3, 0)
-    for n in (0, 2):
-        for d in (1, 3, 2):
-            back_pair(n, d)
-            back_pair(n + 1, d)
-    landed(out_u.at[0:384], r_ubx)
+    for d in (1, 3, 2):
+        back_pair(0, d)
+        back_pair(1, d)
+    for d in (1, 3, 2):
+        back_pair(2, d)
+        back_pair(3, d)
+    landed(out_u.at[0:128], r_uh)
     landed(out_q.at[:, others], r_qc)
     landed(out_r.at[:, others], r_pair)
     left(stat_in, 0)
@@ -465,8 +526,11 @@
             left(gr.at[0 : sent[s]], s)
 
 
+KINDS = ("join", "one", "two", "three", "z", "s1", "s2", "s3", "h1", "h3") + tuple(
+    f"f{d}_{k}" for d in (1, 3) for k in range(4)
+)
 SENDS = 16
-RECVS = 56
+RECVS = 92
 
 
 def per_device(user_states, quot_rows, rem_table, neg_rem, pos_quot, pos_rem):
@@ -503,6 +567,7 @@
             pltpu.VMEM((8, 128), F32),
             pltpu.VMEM((2, NN, H), F32),
             pltpu.VMEM((NN, H), F32),
+            pltpu.VMEM((256, NN + 2 * NU), BF16),
             pltpu.VMEM((NN + 2 * NU, D), BF16),
             pltpu.VMEM((2 * NU, D), BF16),
             pltpu.VMEM((NR, H), F32),

time: 80 us -> 78 us (0.975)
  Pallas kernels: 75.4 us -> 73.5 us
    pallas_call x1, Pallas kernels: 75.4 us -> 73.5 us  [per_device(): pl.pallas_call(kernel, out_shape=(pltpu.VMEM((NU, D), F32), pltpu.VMEM((N...]
where the time goes in v4:
time: 78 us; the launch traced here: 77.9 us
  Pallas kernels  73.5 us (94%)
  local copies, waits for them, and re-layouts  3.78 us (5%)
    pallas_call x1, Pallas kernels, per_device(): pl.pallas_call(kernel, out_shape=(pltpu.VMEM((NU, D), F32), pltpu.VMEM((N...  73.5 us
    unnamed x3, local copies, waits for them, and re-layouts  3.78 us

profile of v4, /device:TPU:1, one launch (start us, length us, event | category | flops | bytes accessed | tf_op | source)
XLA Modules:
  0.0 77.9 jit_solution(10628253989681922629)
XLA Ops:
  0.6 73.5 %sampled_softmax_grads.1 = (f32[512,256]{1,0:T(8,128)S(1)}, f32[1024,256]{1,0:T(8,128)S(1)}, f32[4096,256]{1,0:T(8,128)S(1)}) custom-call(bf16[512,256]{1,0:T(8,128)(2,1)} %user_hbm.1, bf16[1024,256]{1,0:T(8,128)(2,1)} %quot_hbm.1, bf16[4096,256]{1,0:T(8,128)(2,1)} %rem_hbm.1, s32[1,1024]{1,0:T(1,128)} %bitcast.3, s32[1,512]{1,0:T(1,128)} %bitcast.4, ...), custom_call_target="tpu_custom_call" | custom-call | flops 12884901888 | bytes 9437184 | tf_op jit(solution)/shard_map/sampled_softmax_grads/pallas_call | solution.py:539
  74.1 0.8 %copy.12 = f32[512,256]{1,0:T(8,128)} copy(f32[512,256]{1,0:T(8,128)S(1)} %get-tuple-element.3) | data formatting | bytes 1048576
  74.9 1.0 %copy.13 = f32[1024,256]{1,0:T(8,128)} copy(f32[1024,256]{1,0:T(8,128)S(1)} %get-tuple-element.4) | data formatting | bytes 2097152
  75.9 2.0 %copy.14 = f32[4096,256]{1,0:T(8,128)} copy(f32[4096,256]{1,0:T(8,128)S(1)} %get-tuple-element.5) | data formatting | bytes 8388608

commit v5 on v4

--- a/solution.py
+++ b/solution.py
@@ -413,10 +413,12 @@
         to_pair(at)
 
     for d in order:
-        one(0, d)
-        one(1, d)
+        for n in range(4):
+            one(n, d)
     join(0)
     join(1)
+    join(2)
+    join(3)
     ru = x * 128
     landed(u1, r_ux)
     lse_mine = scales[pl.ds(x, 1), :]
@@ -434,15 +436,17 @@
     r_uz = slot()
     for d in (2, 1, 3):
         go(mid.at[rows(((zh + d) % 4) * 32, 32)], u2.at[d - 1], peer(dz=2 * d), 14, r_uz, 64)
-    for d in order:
-        one(2, d)
-        one(3, d)
-    join(2)
-    join(3)
     two(0)
     two(1)
     two(2)
     two(3)
+    ru2 = ru + zh * 32
+    landed(u2, r_uz)
+    out_u[rows(ru2, 32), :] = fold(mid, zh * 32, 32, u2, 3)
+    r_ubz = slot()
+    for d in (2, 1, 3):
+        at = rows(ru2, 32)
+        go(out_u.at[at], out_u.at[at], peer(dz=2 * d), 14, r_ubz, 64)
     landed(q1, r_qz)
     gq[rows(rq, 512), :] = fold(gq, rq, 512, q1, 1)
     r_qy = slot()
@@ -451,15 +455,13 @@
         go(gq.at[at], q2.at[d - 1], peer(dy=d), 15, r_qy, 128)
     three(0)
     three(1)
-    ru2 = ru + zh * 32
-    landed(u2, r_uz)
-    out_u[rows(ru2, 32), :] = fold(mid, zh * 32, 32, u2, 3)
-    r_ubz = slot()
-    for d in (2, 1, 3):
-        at = rows(ru2, 32)
-        go(out_u.at[at], out_u.at[at], peer(dz=2 * d), 14, r_ubz, 64)
     three(2)
     three(3)
+    landed(out_u.at[0:96], r_ubz)
+    r_ub1, r_ub3, r_uh = slot(), slot(), slot()
+    at = rows(ru, 128)
+    go(out_u.at[at], out_u.at[at], peer(dx=1), 14, r_ub1, 256)
+    go(out_u.at[at], out_u.at[at], peer(dx=3), 14, r_ub3, 256)
     rq2 = rq + y * 128
     landed(q2, r_qy)
     out_q[rows(rq2, 128), mine] = fold(gq, rq2, 128, q2, 3)
@@ -471,11 +473,6 @@
     back_z(1)
     back_z(2)
     back_z(3)
-    landed(out_u.at[0:96], r_ubz)
-    r_ub1, r_ub3, r_uh = slot(), slot(), slot()
-    at = rows(ru, 128)
-    go(out_u.at[at], out_u.at[at], peer(dx=1), 14, r_ub1, 256)
-    go(out_u.at[at], out_u.at[at], peer(dx=3), 14, r_ub3, 256)
     landed(out_q.at[0:384, mine], r_qby)
     r_qbz, r_qc = slot(), slot()
     at = rows(rq, 512)
@@ -485,10 +482,6 @@
     back_second(1)
     back_second(2)
     back_second(3)
-    pass_on(0, 0)
-    pass_on(1, 0)
-    pass_on(2, 0)
-    pass_on(3, 0)
     for d, h, r in ((1, 0, r_ub1), (3, 64, r_ub3)):
         r0 = ((x - d) % 4) * 128
         landed(out_u.at[rows(r0, 128)], r)
@@ -498,25 +491,26 @@
     back_first(1)
     back_first(2)
     back_first(3)
-    back_pair(0, 0)
-    back_pair(1, 0)
-    back_pair(2, 0)
-    back_pair(3, 0)
+    pass_on(0, 0)
+    pass_on(1, 0)
+    pass_on(2, 0)
+    pass_on(3, 0)
     for k in (1, 3, 2):
         pass_on(0, k)
         pass_on(1, k)
     for k in (1, 3, 2):
         pass_on(2, k)
         pass_on(3, k)
+    back_pair(0, 0)
+    back_pair(1, 0)
+    back_pair(2, 0)
+    back_pair(3, 0)
     at = rows((1 - zl) * 512, 512)
     landed(out_q.at[at, mine], r_qbz)
     go(out_q.at[at, mine], out_q.at[at, mine], peer(dc=1), 15, r_qc, 512)
     for d in (1, 3, 2):
-        back_pair(0, d)
-        back_pair(1, d)
-    for d in (1, 3, 2):
-        back_pair(2, d)
-        back_pair(3, d)
+        for n in range(4):
+            back_pair(n, d)
     landed(out_u.at[0:128], r_uh)
     landed(out_q.at[:, others], r_qc)
     landed(out_r.at[:, others], r_pair)

time: 78 us -> 75.7 us (0.971)
  Pallas kernels: 73.5 us -> 71.1 us
    pallas_call x1, Pallas kernels: 73.5 us -> 71.1 us  [per_device(): pl.pallas_call(kernel, out_shape=(pltpu.VMEM((NU, D), F32), pltpu.VMEM((N...]
where the time goes in v5:
time: 75.7 us; the launch traced here: 75.6 us
  Pallas kernels  71.1 us (94%)
  local copies, waits for them, and re-layouts  3.78 us (5%)
    pallas_call x1, Pallas kernels, per_device(): pl.pallas_call(kernel, out_shape=(pltpu.VMEM((NU, D), F32), pltpu.VMEM((N...  71.1 us
    unnamed x3, local copies, waits for them, and re-layouts  3.78 us

profile of v5, /device:TPU:1, one launch (start us, length us, event | category | flops | bytes accessed | tf_op | source)
XLA Modules:
  0.0 75.6 jit_solution(15904534699638948129)
XLA Ops:
  0.6 71.1 %sampled_softmax_grads.1 = (f32[512,256]{1,0:T(8,128)S(1)}, f32[1024,256]{1,0:T(8,128)S(1)}, f32[4096,256]{1,0:T(8,128)S(1)}) custom-call(bf16[512,256]{1,0:T(8,128)(2,1)} %user_hbm.1, bf16[1024,256]{1,0:T(8,128)(2,1)} %quot_hbm.1, bf16[4096,256]{1,0:T(8,128)(2,1)} %rem_hbm.1, s32[1,1024]{1,0:T(1,128)} %bitcast.3, s32[1,512]{1,0:T(1,128)} %bitcast.4, ...), custom_call_target="tpu_custom_call" | custom-call | flops 12884901888 | bytes 9437184 | tf_op jit(solution)/shard_map/sampled_softmax_grads/pallas_call | solution.py:533
  71.8 0.8 %copy.12 = f32[512,256]{1,0:T(8,128)} copy(f32[512,256]{1,0:T(8,128)S(1)} %get-tuple-element.3) | data formatting | bytes 1048576
  72.6 1.0 %copy.13 = f32[1024,256]{1,0:T(8,128)} copy(f32[1024,256]{1,0:T(8,128)S(1)} %get-tuple-element.4) | data formatting | bytes 2097152
  73.5 2.0 %copy.14 = f32[4096,256]{1,0:T(8,128)} copy(f32[4096,256]{1,0:T(8,128)S(1)} %get-tuple-element.5) | data formatting | bytes 8388608
